TPU v7x, 32 devices: a whole 2x2x4 slice. The times are simulated.
32 devices in a mesh: ctx: 16 (over z, y, x), head: 2 (over core).
Axes of the slice: x: 2, y: 2, z: 4, core: 2. Of those that a mesh axis runs over, the one named last changes fastest.
Arguments:
- query_rows: bfloat16 [8192, 512], P('ctx', 'head'), parts along dimension 1, may hold values from -6 to 6
- key_rows: bfloat16 [8192, 512], P('ctx', 'head'), parts along dimension 1, may hold values from -6 to 6
- value_rows: bfloat16 [8192, 512], P('ctx', 'head'), parts along dimension 1, may hold values from -6 to 6
- out_grad: bfloat16 [8192, 512], P('ctx', 'head'), parts along dimension 1, may hold values from -6 to 6
- doc_lengths: int32 [16], P('head'), parts along dimension 0, may hold values from 1 to 2048, 8192 in all
Outputs:
- attended: bfloat16 [8192, 512], P('ctx', 'head'), parts along dimension 1
- grad_query: bfloat16 [8192, 512], P('ctx', 'head'), parts along dimension 1
- grad_key: bfloat16 [8192, 512], P('ctx', 'head'), parts along dimension 1
- grad_value: bfloat16 [8192, 512], P('ctx', 'head'), parts along dimension 1
There are 2 independent parts, one for each index of `head`. A program takes and returns all parts, laid end to end along the dimension named above; each array names one. Nothing has to cross between parts.
Inputs may be any that keep to these rules, and one draw needn't show every extreme that they name: `doc_lengths`: the lengths add up to 8192; the longest document holds exactly 2048 tokens.
All inputs are finite; a program needn't handle non-finite values.
Results may differ from a plain program's by a relative error of at most 0.0051.
Values sent between devices are 32-bit elements; how exact they have to be, the bound alone decides.
No kernel may reach another device: no remote copies, remote signals or barrier semaphores. Data moves between devices by JAX's collectives and lax.ppermute only.
A program may use at most 64 MiB of HBM per device.

v0:
```python
import jax
import jax.numpy as jnp
from jax import lax
from jax.sharding import PartitionSpec as P

HD = 128


def shifted(value, axis, steps):
    count = lax.axis_size(axis)
    initial, last = (max(0, -steps), min(count, count - steps))
    return lax.ppermute(value, axis, [(source, source + steps) for source in range(initial, last)])


def doc_layout(doc_lengths, base, rows):
    count = doc_lengths.shape[0]
    starts = jnp.cumsum(doc_lengths) - doc_lengths
    finish = starts + doc_lengths
    positions = base + jnp.arange(rows, dtype=jnp.int32)
    member = (
        (positions[:, None] >= starts[None, :]) & (positions[:, None] < finish[None, :])
    ).astype(jnp.int32)
    labels = jnp.arange(count, dtype=jnp.int32)
    doc_index = jnp.sum(member * labels[None, :], axis=1)
    offsets = positions - jnp.sum(member * starts[None, :], axis=1)
    first_doc = doc_index[0]
    last_doc = doc_index[rows - 1]
    first_start = jnp.sum(jnp.where(labels == first_doc, starts, 0))
    last_start = jnp.sum(jnp.where(labels == last_doc, starts, 0))
    first_finish = jnp.sum(jnp.where(labels == first_doc, finish, 0))
    last_finish = jnp.sum(jnp.where(labels == last_doc, finish, 0))
    carry_in = (first_start < base).astype(jnp.float32)
    reset_fwd = (last_start >= base).astype(jnp.float32)
    reset_bwd = (first_finish <= base + rows).astype(jnp.float32)
    carry_back = (last_finish > base + rows).astype(jnp.float32)
    local = jnp.arange(rows, dtype=jnp.int32)
    allowed = (doc_index[:, None] == doc_index[None, :]) & (local[:, None] >= local[None, :])
    return (
        offsets,
        doc_index == first_doc,
        doc_index == last_doc,
        carry_in,
        reset_fwd,
        reset_bwd,
        carry_back,
        allowed,
    )


def body(query_rows, key_rows, value_rows, out_grad, doc_lengths):
    hi = lax.Precision.HIGHEST
    rows = query_rows.shape[0]
    head_dim = HD
    heads = query_rows.shape[1] // head_dim
    base = lax.axis_index("ctx") * rows
    layout = doc_layout(doc_lengths, base, rows)
    offsets, first_rows, last_rows, carry_in, reset_fwd, reset_bwd, carry_back, allowed = layout
    row_scale = lax.rsqrt(offsets.astype(jnp.float32) + 1.0) * head_dim ** (-0.5)
    query_heads = query_rows.reshape(rows, heads, head_dim)
    key_heads = key_rows.reshape(rows, heads, head_dim)
    value_heads = value_rows.reshape(rows, heads, head_dim)
    grad_heads = out_grad.reshape(rows, heads, head_dim)
    scaled = (query_heads.astype(jnp.float32) * row_scale[:, None, None]).astype(jnp.bfloat16)
    tail_keys = jnp.where(last_rows[:, None, None], key_heads, jnp.zeros_like(key_heads))
    tail_state = jnp.einsum(
        "thd,the->hde", tail_keys, value_heads, preferred_element_type=jnp.float32
    )
    head_queries = jnp.where(first_rows[:, None, None], scaled, jnp.zeros_like(scaled))
    head_state = jnp.einsum(
        "thd,the->hde", head_queries, grad_heads, preferred_element_type=jnp.float32
    )
    zero_state = jnp.zeros((heads, head_dim, head_dim), jnp.float32)
    reach = lax.axis_size("ctx") // 4

    def pass_forward(step_no, carry):
        received = shifted(carry[0], "ctx", 1)
        return (tail_state + (1.0 - reset_fwd) * received, received)

    def pass_backward(step_no, carry):
        received = shifted(carry[0], "ctx", -1)
        return (head_state + (1.0 - reset_bwd) * received, received)

    fwd_carry = lax.fori_loop(0, reach, pass_forward, (tail_state, zero_state))
    bwd_carry = lax.fori_loop(0, reach, pass_backward, (head_state, zero_state))
    entering = fwd_carry[1] * carry_in
    returning = bwd_carry[1] * carry_back
    mask_heads = allowed[None, :, :]
    scores = jnp.einsum("thd,shd->hts", scaled, key_heads, preferred_element_type=jnp.float32)
    weights = jnp.where(mask_heads, scores, 0.0).astype(jnp.bfloat16)
    dscores = jnp.einsum(
        "the,she->hts", grad_heads, value_heads, preferred_element_type=jnp.float32
    )
    dweights = jnp.where(mask_heads, dscores, 0.0).astype(jnp.bfloat16)
    attended = jnp.einsum("thd,hde->the", scaled.astype(jnp.float32), entering, precision=hi)
    attended = attended + jnp.einsum(
        "hts,she->the", weights, value_heads, preferred_element_type=jnp.float32
    )
    grad_q = jnp.einsum("the,hde->thd", grad_heads.astype(jnp.float32), entering, precision=hi)
    grad_q = row_scale[:, None, None] * (
        grad_q + jnp.einsum("hts,shd->thd", dweights, key_heads, preferred_element_type=jnp.float32)
    )
    grad_k = jnp.einsum("she,hde->shd", value_heads.astype(jnp.float32), returning, precision=hi)
    grad_k = grad_k + jnp.einsum(
        "hts,thd->shd", dweights, scaled, preferred_element_type=jnp.float32
    )
    grad_v = jnp.einsum("shd,hde->she", key_heads.astype(jnp.float32), returning, precision=hi)
    grad_v = grad_v + jnp.einsum(
        "hts,the->she", weights, grad_heads, preferred_element_type=jnp.float32
    )
    flat = (rows, heads * head_dim)
    return (
        attended.astype(jnp.bfloat16).reshape(flat),
        grad_q.astype(jnp.bfloat16).reshape(flat),
        grad_k.astype(jnp.bfloat16).reshape(flat),
        grad_v.astype(jnp.bfloat16).reshape(flat),
    )


def solution(mesh):
    in_specs = (P("ctx", "head"), P("ctx", "head"), P("ctx", "head"), P("ctx", "head"), P("head"))
    out_specs = (P("ctx", "head"), P("ctx", "head"), P("ctx", "head"), P("ctx", "head"))
    return jax.shard_map(body, mesh=mesh, in_specs=in_specs, out_specs=out_specs, check_vma=False)
```

profile of v0, /device:TPU:24, one launch (start us, length us, event | category | flops | bytes accessed | tf_op | source)
XLA Modules:
  0.0 96.0 jit_solution(624572172028937106)
XLA Ops:
  0.7 0.9 reduce-window.8
  2.9 1.3 %broadcast_compare_fusion = (pred[512]{0:T(512)(128)(4,1)S(1)}, pred[512]{0:T(512)(128)(4,1)S(1)}) fusion(s32[512]{0:T(512)S(1)} %get-tuple-element.130, s32[]{:T(128)} %bitcast.4, s32[]{:T(128)} %bitcast.2), kind=kLoop, calls=%fused_computation.56 | loop fusion | flops 1024 | bytes 3080 | tf_op jit(solution)/shard_map/eq | solution.py:40
  4.2 1.1 %copy.31 = f32[512,256]{0,1:T(8,128)S(1)} copy(bf16[512,256]{1,0:T(8,128)(2,1)} %param.9) | data formatting | bytes 786432 | tf_op jit(solution)/shard_map/convert_element_type | solution.py:63
  5.8 2.0 %fusion.35 = (s32[]{:T(128)}, s32[]{:T(128)}, s32[]{:T(128)}, s32[]{:T(128)}) fusion(s32[]{:T(128)} %bitcast.2, s32[8,1]{0,1:T(1,128)S(1)} %reduce-window.8, s32[]{:T(128)} %bitcast.4, s32[8]{0:T(128)S(1)} %bitcast_subtract_fusion), kind=kLoop, calls=%fused_computation.59 | loop fusion | flops 76 | bytes 88 | tf_op jit(solution)/shard_map/reduce_sum | solution.py:31
  9.1 35.7 %while.29 = (s32[]{:T(128)}, f32[2,128,128]{2,1,0:T(8,128)S(1)}, f32[2,128,128]{2,1,0:T(8,128)}, f32[]{:T(128)}, f32[2,128,128]{2,1,0:T(8,128)S(1)}, /*index=5*/s32[]{:T(128)}) while((s32[]{:T(128)}, f32[2,128,128]{2,1,0:T(8,128)S(1)}, f32[2,128,128]{2,1,0:T(8,128)}, f32[]{:T(128)}, f32[2,128,128]{2,1,0:T(8,128)S(1)}, ...), condition=%wide.region_9.10_spmd, body=%wide.region_8.9_spmd.sunk | while | flops 65538 | bytes 1441933 | solution.py:84
  9.1 4.4 %collective-permute-start.1 = (f32[2,128,128]{2,1,0:T(8,128)S(1)}, f32[2,128,128]{2,1,0:T(8,128)S(1)}, u32[]{:S(2)}, u32[]{:S(2)}) collective-permute-start(f32[2,128,128]{2,1,0:T(8,128)S(1)} %get-tuple-element.245), channel_id=1, source_target_pairs={{2,0},{4,2},{6,4},{8,6},{10,8},{12,10},{14,12},{16,14},{18,16},{20... | collective-permute-start | bytes 393224 | tf_op jit(solution)/shard_map/while/body/eval_jaxpr/ppermute | solution.py:12
  13.5 2.9 %collective-permute-done.1 = f32[2,128,128]{2,1,0:T(8,128)S(1)} collective-permute-done((f32[2,128,128]{2,1,0:T(8,128)S(1)}, f32[2,128,128]{2,1,0:T(8,128)S(1)}, u32[]{:S(2)}, u32[]{:S(2)}) %collective-permute-start.1) | collective-permute-done | bytes 131104 | tf_op jit(solution)/shard_map/while/body/eval_jaxpr/ppermute | solution.py:12
  17.0 6.0 %collective-permute-start.1 = (f32[2,128,128]{2,1,0:T(8,128)S(1)}, f32[2,128,128]{2,1,0:T(8,128)S(1)}, u32[]{:S(2)}, u32[]{:S(2)}) collective-permute-start(f32[2,128,128]{2,1,0:T(8,128)S(1)} %get-tuple-element.245), channel_id=1, source_target_pairs={{2,0},{4,2},{6,4},{8,6},{10,8},{12,10},{14,12},{16,14},{18,16},{20... | collective-permute-start | bytes 393224 | tf_op jit(solution)/shard_map/while/body/eval_jaxpr/ppermute | solution.py:12
  23.1 2.5 %collective-permute-done.1 = f32[2,128,128]{2,1,0:T(8,128)S(1)} collective-permute-done((f32[2,128,128]{2,1,0:T(8,128)S(1)}, f32[2,128,128]{2,1,0:T(8,128)S(1)}, u32[]{:S(2)}, u32[]{:S(2)}) %collective-permute-start.1) | collective-permute-done | bytes 131104 | tf_op jit(solution)/shard_map/while/body/eval_jaxpr/ppermute | solution.py:12
  26.2 6.1 %collective-permute-start.1 = (f32[2,128,128]{2,1,0:T(8,128)S(1)}, f32[2,128,128]{2,1,0:T(8,128)S(1)}, u32[]{:S(2)}, u32[]{:S(2)}) collective-permute-start(f32[2,128,128]{2,1,0:T(8,128)S(1)} %get-tuple-element.245), channel_id=1, source_target_pairs={{2,0},{4,2},{6,4},{8,6},{10,8},{12,10},{14,12},{16,14},{18,16},{20... | collective-permute-start | bytes 393224 | tf_op jit(solution)/shard_map/while/body/eval_jaxpr/ppermute | solution.py:12
  32.4 2.5 %collective-permute-done.1 = f32[2,128,128]{2,1,0:T(8,128)S(1)} collective-permute-done((f32[2,128,128]{2,1,0:T(8,128)S(1)}, f32[2,128,128]{2,1,0:T(8,128)S(1)}, u32[]{:S(2)}, u32[]{:S(2)}) %collective-permute-start.1) | collective-permute-done | bytes 131104 | tf_op jit(solution)/shard_map/while/body/eval_jaxpr/ppermute | solution.py:12
  35.5 6.1 %collective-permute-start.1 = (f32[2,128,128]{2,1,0:T(8,128)S(1)}, f32[2,128,128]{2,1,0:T(8,128)S(1)}, u32[]{:S(2)}, u32[]{:S(2)}) collective-permute-start(f32[2,128,128]{2,1,0:T(8,128)S(1)} %get-tuple-element.245), channel_id=1, source_target_pairs={{2,0},{4,2},{6,4},{8,6},{10,8},{12,10},{14,12},{16,14},{18,16},{20... | collective-permute-start | bytes 393224 | tf_op jit(solution)/shard_map/while/body/eval_jaxpr/ppermute | solution.py:12
  41.7 2.5 %collective-permute-done.1 = f32[2,128,128]{2,1,0:T(8,128)S(1)} collective-permute-done((f32[2,128,128]{2,1,0:T(8,128)S(1)}, f32[2,128,128]{2,1,0:T(8,128)S(1)}, u32[]{:S(2)}, u32[]{:S(2)}) %collective-permute-start.1) | collective-permute-done | bytes 131104 | tf_op jit(solution)/shard_map/while/body/eval_jaxpr/ppermute | solution.py:12
  45.7 1.3 %convolution_bitcast_fusion.1 = f32[512,2,128]{0,2,1:T(8,128)S(1)} fusion(bf16[512,2,128]{0,2,1:T(8,128)(2,1)S(1)} %bitcast.78, f32[2,128,128]{2,1,0:T(8,128)} %get-tuple-element.121, f32[]{:T(128)S(6)} %convert_element_type.65), kind=kOutput, calls=%fused_computation.7 | convolution fusion | flops 201359360 | bytes 917508 | tf_op jit(solution)/shard_map/shd,hde->she/dot_general | solution.py:106
  52.5 38.4 %while.28 = (s32[]{:T(128)}, f32[2,128,128]{2,1,0:T(8,128)S(1)}, f32[2,128,128]{2,1,0:T(8,128)}, f32[]{:T(128)}, f32[2,128,128]{2,1,0:T(8,128)S(1)}, /*index=5*/s32[]{:T(128)}) while((s32[]{:T(128)}, f32[2,128,128]{2,1,0:T(8,128)S(1)}, f32[2,128,128]{2,1,0:T(8,128)}, f32[]{:T(128)}, f32[2,128,128]{2,1,0:T(8,128)S(1)}, ...), condition=%wide.region_4.5_spmd, body=%wide.region_3.4_spmd.sunk | while | flops 65538 | bytes 1441933 | solution.py:83
  52.5 1.9 %collective-permute-start = (f32[2,128,128]{2,1,0:T(8,128)S(1)}, f32[2,128,128]{2,1,0:T(8,128)S(1)}, u32[]{:S(2)}, u32[]{:S(2)}) collective-permute-start(f32[2,128,128]{2,1,0:T(8,128)S(1)} %get-tuple-element.227), channel_id=1, source_target_pairs={{0,2},{2,4},{4,6},{6,8},{8,10},{10,12},{12,14},{14,16},{16,18},{18... | collective-permute-start | bytes 393224 | tf_op jit(solution)/shard_map/while/body/eval_jaxpr/ppermute | solution.py:12
  54.4 7.2 %collective-permute-done = f32[2,128,128]{2,1,0:T(8,128)S(1)} collective-permute-done((f32[2,128,128]{2,1,0:T(8,128)S(1)}, f32[2,128,128]{2,1,0:T(8,128)S(1)}, u32[]{:S(2)}, u32[]{:S(2)}) %collective-permute-start) | collective-permute-done | bytes 131104 | tf_op jit(solution)/shard_map/while/body/eval_jaxpr/ppermute | solution.py:12
  62.2 1.9 %collective-permute-start = (f32[2,128,128]{2,1,0:T(8,128)S(1)}, f32[2,128,128]{2,1,0:T(8,128)S(1)}, u32[]{:S(2)}, u32[]{:S(2)}) collective-permute-start(f32[2,128,128]{2,1,0:T(8,128)S(1)} %get-tuple-element.227), channel_id=1, source_target_pairs={{0,2},{2,4},{4,6},{6,8},{8,10},{10,12},{12,14},{14,16},{16,18},{18... | collective-permute-start | bytes 393224 | tf_op jit(solution)/shard_map/while/body/eval_jaxpr/ppermute | solution.py:12
  64.1 6.7 %collective-permute-done = f32[2,128,128]{2,1,0:T(8,128)S(1)} collective-permute-done((f32[2,128,128]{2,1,0:T(8,128)S(1)}, f32[2,128,128]{2,1,0:T(8,128)S(1)}, u32[]{:S(2)}, u32[]{:S(2)}) %collective-permute-start) | collective-permute-done | bytes 131104 | tf_op jit(solution)/shard_map/while/body/eval_jaxpr/ppermute | solution.py:12
  71.5 1.9 %collective-permute-start = (f32[2,128,128]{2,1,0:T(8,128)S(1)}, f32[2,128,128]{2,1,0:T(8,128)S(1)}, u32[]{:S(2)}, u32[]{:S(2)}) collective-permute-start(f32[2,128,128]{2,1,0:T(8,128)S(1)} %get-tuple-element.227), channel_id=1, source_target_pairs={{0,2},{2,4},{4,6},{6,8},{8,10},{10,12},{12,14},{14,16},{16,18},{18... | collective-permute-start | bytes 393224 | tf_op jit(solution)/shard_map/while/body/eval_jaxpr/ppermute | solution.py:12
  73.4 7.5 %collective-permute-done = f32[2,128,128]{2,1,0:T(8,128)S(1)} collective-permute-done((f32[2,128,128]{2,1,0:T(8,128)S(1)}, f32[2,128,128]{2,1,0:T(8,128)S(1)}, u32[]{:S(2)}, u32[]{:S(2)}) %collective-permute-start) | collective-permute-done | bytes 131104 | tf_op jit(solution)/shard_map/while/body/eval_jaxpr/ppermute | solution.py:12
  81.6 1.9 %collective-permute-start = (f32[2,128,128]{2,1,0:T(8,128)S(1)}, f32[2,128,128]{2,1,0:T(8,128)S(1)}, u32[]{:S(2)}, u32[]{:S(2)}) collective-permute-start(f32[2,128,128]{2,1,0:T(8,128)S(1)} %get-tuple-element.227), channel_id=1, source_target_pairs={{0,2},{2,4},{4,6},{6,8},{8,10},{10,12},{12,14},{14,16},{16,18},{18... | collective-permute-start | bytes 393224 | tf_op jit(solution)/shard_map/while/body/eval_jaxpr/ppermute | solution.py:12
  83.5 6.7 %collective-permute-done = f32[2,128,128]{2,1,0:T(8,128)S(1)} collective-permute-done((f32[2,128,128]{2,1,0:T(8,128)S(1)}, f32[2,128,128]{2,1,0:T(8,128)S(1)}, u32[]{:S(2)}, u32[]{:S(2)}) %collective-permute-start) | collective-permute-done | bytes 131104 | tf_op jit(solution)/shard_map/while/body/eval_jaxpr/ppermute | solution.py:12
  91.6 1.3 %convolution_bitcast_fusion.3 = f32[512,2,128]{0,2,1:T(8,128)S(1)} fusion(bf16[512,2,128]{0,2,1:T(8,128)(2,1)S(1)} %bitcast.85, f32[2,128,128]{2,1,0:T(8,128)} %get-tuple-element.120, f32[]{:T(128)S(6)} %convert_element_type.55), kind=kOutput, calls=%fused_computation.11 | convolution fusion | flops 201359360 | bytes 917508 | tf_op jit(solution)/shard_map/the,hde->thd/dot_general | solution.py:98
  (61 shorter events, 15.7 us)
Async XLA Ops:
  0.6 48.3 %copy-start = (bf16[512,256]{1,0:T(8,128)(2,1)S(1)}, bf16[512,256]{1,0:T(8,128)(2,1)}, u32[]{:S(2)}) copy-start(bf16[512,256]{1,0:T(8,128)(2,1)} %param.11) | copy-start | bytes 786436
  0.6 4.7 %copy-start.5 = (bf16[512,256]{1,0:T(8,128)(2,1)S(1)}, bf16[512,256]{1,0:T(8,128)(2,1)}, u32[]{:S(2)}) copy-start(bf16[512,256]{1,0:T(8,128)(2,1)} %param.12) | copy-start | bytes 786436
  9.1 36.4 %copy-start.6 = (bf16[512,256]{1,0:T(8,128)(2,1)S(1)}, bf16[512,256]{1,0:T(8,128)(2,1)}, u32[]{:S(2)}) copy-start(bf16[512,256]{1,0:T(8,128)(2,1)} %param.10) | copy-start | bytes 786436
  9.1 7.2 %collective-permute-start.1 = (f32[2,128,128]{2,1,0:T(8,128)S(1)}, f32[2,128,128]{2,1,0:T(8,128)S(1)}, u32[]{:S(2)}, u32[]{:S(2)}) collective-permute-start(f32[2,128,128]{2,1,0:T(8,128)S(1)} %get-tuple-element.245), channel_id=1, source_target_pairs={{2,0},{4,2},{6,4},{8,6},{10,8},{12,10},{14,12},{16,14},{18,16},{20... | collective-permute-start | bytes 393224 | tf_op jit(solution)/shard_map/while/body/eval_jaxpr/ppermute | solution.py:12
  16.4 0.7 copy-start.3
  17.0 8.5 %collective-permute-start.1 = (f32[2,128,128]{2,1,0:T(8,128)S(1)}, f32[2,128,128]{2,1,0:T(8,128)S(1)}, u32[]{:S(2)}, u32[]{:S(2)}) collective-permute-start(f32[2,128,128]{2,1,0:T(8,128)S(1)} %get-tuple-element.245), channel_id=1, source_target_pairs={{2,0},{4,2},{6,4},{8,6},{10,8},{12,10},{14,12},{16,14},{18,16},{20... | collective-permute-start | bytes 393224 | tf_op jit(solution)/shard_map/while/body/eval_jaxpr/ppermute | solution.py:12
  25.6 0.7 copy-start.3
  26.2 8.6 %collective-permute-start.1 = (f32[2,128,128]{2,1,0:T(8,128)S(1)}, f32[2,128,128]{2,1,0:T(8,128)S(1)}, u32[]{:S(2)}, u32[]{:S(2)}) collective-permute-start(f32[2,128,128]{2,1,0:T(8,128)S(1)} %get-tuple-element.245), channel_id=1, source_target_pairs={{2,0},{4,2},{6,4},{8,6},{10,8},{12,10},{14,12},{16,14},{18,16},{20... | collective-permute-start | bytes 393224 | tf_op jit(solution)/shard_map/while/body/eval_jaxpr/ppermute | solution.py:12
  34.9 0.7 copy-start.3
  35.5 8.6 %collective-permute-start.1 = (f32[2,128,128]{2,1,0:T(8,128)S(1)}, f32[2,128,128]{2,1,0:T(8,128)S(1)}, u32[]{:S(2)}, u32[]{:S(2)}) collective-permute-start(f32[2,128,128]{2,1,0:T(8,128)S(1)} %get-tuple-element.245), channel_id=1, source_target_pairs={{2,0},{4,2},{6,4},{8,6},{10,8},{12,10},{14,12},{16,14},{18,16},{20... | collective-permute-start | bytes 393224 | tf_op jit(solution)/shard_map/while/body/eval_jaxpr/ppermute | solution.py:12
  44.2 0.7 copy-start.3
  47.7 1.2 %copy-start.4 = (f32[2,128,128]{2,1,0:T(8,128)S(1)}, f32[2,128,128]{2,1,0:T(8,128)}, u32[]{:S(2)}) copy-start(f32[2,128,128]{2,1,0:T(8,128)} %get-tuple-element.121) | copy-start | bytes 393220
  52.5 9.1 %collective-permute-start = (f32[2,128,128]{2,1,0:T(8,128)S(1)}, f32[2,128,128]{2,1,0:T(8,128)S(1)}, u32[]{:S(2)}, u32[]{:S(2)}) collective-permute-start(f32[2,128,128]{2,1,0:T(8,128)S(1)} %get-tuple-element.227), channel_id=1, source_target_pairs={{0,2},{2,4},{4,6},{6,8},{8,10},{10,12},{12,14},{14,16},{16,18},{18... | collective-permute-start | bytes 393224 | tf_op jit(solution)/shard_map/while/body/eval_jaxpr/ppermute | solution.py:12
  61.5 0.7 copy-start.1
  62.2 8.6 %collective-permute-start = (f32[2,128,128]{2,1,0:T(8,128)S(1)}, f32[2,128,128]{2,1,0:T(8,128)S(1)}, u32[]{:S(2)}, u32[]{:S(2)}) collective-permute-start(f32[2,128,128]{2,1,0:T(8,128)S(1)} %get-tuple-element.227), channel_id=1, source_target_pairs={{0,2},{2,4},{4,6},{6,8},{8,10},{10,12},{12,14},{14,16},{16,18},{18... | collective-permute-start | bytes 393224 | tf_op jit(solution)/shard_map/while/body/eval_jaxpr/ppermute | solution.py:12
  70.9 0.7 copy-start.1
  71.5 9.4 %collective-permute-start = (f32[2,128,128]{2,1,0:T(8,128)S(1)}, f32[2,128,128]{2,1,0:T(8,128)S(1)}, u32[]{:S(2)}, u32[]{:S(2)}) collective-permute-start(f32[2,128,128]{2,1,0:T(8,128)S(1)} %get-tuple-element.227), channel_id=1, source_target_pairs={{0,2},{2,4},{4,6},{6,8},{8,10},{10,12},{12,14},{14,16},{16,18},{18... | collective-permute-start | bytes 393224 | tf_op jit(solution)/shard_map/while/body/eval_jaxpr/ppermute | solution.py:12
  80.9 0.7 copy-start.1
  81.6 8.6 %collective-permute-start = (f32[2,128,128]{2,1,0:T(8,128)S(1)}, f32[2,128,128]{2,1,0:T(8,128)S(1)}, u32[]{:S(2)}, u32[]{:S(2)}) collective-permute-start(f32[2,128,128]{2,1,0:T(8,128)S(1)} %get-tuple-element.227), channel_id=1, source_target_pairs={{0,2},{2,4},{4,6},{6,8},{8,10},{10,12},{12,14},{14,16},{16,18},{18... | collective-permute-start | bytes 393224 | tf_op jit(solution)/shard_map/while/body/eval_jaxpr/ppermute | solution.py:12
  90.2 0.7 copy-start.1
  92.9 1.3 %copy-start.2 = (f32[2,128,128]{2,1,0:T(8,128)S(1)}, f32[2,128,128]{2,1,0:T(8,128)}, u32[]{:S(2)}) copy-start(f32[2,128,128]{2,1,0:T(8,128)} %get-tuple-element.120) | copy-start | bytes 393220
where the time goes:
time: 96.4 us; the launch traced here: 96 us
  waiting for transfers between devices  38.5 us (40%)
  starting transfers between devices  30.3 us (31%)
  local copies, waits for them, and re-layouts  11.8 us (12%)
  matrix products  6.48 us (7%)
  other arithmetic  5.37 us (6%)
  between operations  3.41 us (4%)
    ppermute x8, waiting for transfers between devices, shifted(): lax.ppermute(value, axis, [(source, source + steps) for source in range(i...  38.5 us
    ppermute x8, starting transfers between devices, shifted(): lax.ppermute(value, axis, [(source, source + steps) for source in range(i...  30.3 us
    while x16, local copies, waits for them, and re-layouts  5.08 us
    unnamed x17, local copies, waits for them, and re-layouts  3.56 us
    reduce_sum x1, other arithmetic, doc_layout(): last_finish = jnp.sum(jnp.where(labels == last_doc, finish, 0))  2.04 us
  transfers between devices with their start and end apart: 8, of which 8 were waited for; matrix products, arithmetic and copies ran while one was open for 0% of the time, Pallas kernels for 0%

commit v1 on v0

v1 whole, which is shorter than its diff:
```python
import functools

import jax
import jax.numpy as jnp
from jax import lax
from jax.experimental import pallas as pl
from jax.experimental.pallas import tpu as pltpu
from jax.sharding import PartitionSpec as P

HD = 128
F32 = jnp.float32
BF16 = jnp.bfloat16
SMEM = pl.BlockSpec(memory_space=pltpu.SMEM)
VMEM = pl.BlockSpec(memory_space=pltpu.VMEM)


def cycle_within(nodes):
    return [(node, nodes[(at + 1) % len(nodes)]) for at, node in enumerate(nodes)]


def swap_pairs(count, steps):
    pairs = [(j, j + steps) for j in range(1, count - steps, 2)]
    met = {j for pair in pairs for j in pair}
    rest = [j for j in range(count) if j not in met]
    low = [j for j in rest if j < count // 2]
    high = [j for j in rest if j >= count // 2]
    groups = [low, high] if len(low) != 1 and len(high) != 1 else [rest]
    fill = [edge for group in groups for edge in cycle_within(group)]
    return pairs + [(b, a) for a, b in pairs] + fill


def ring_pairs(count, steps):
    out = []
    for j in range(count):
        target = j + steps if j % 2 else j - steps
        if not 0 <= target < count:
            target = j - 1 if j % 2 else j + 1
        out.append((j, target))
    return out


def pair_mates(count):
    return [(j, j ^ 1) for j in range(count)]


def doc_edges(lengths_ref, base, rows):
    first_start = last_start = jnp.int32(0)
    first_finish = last_finish = jnp.int32(2**30)
    start = jnp.int32(0)
    starts = []
    for doc in range(lengths_ref.shape[0]):
        finish = start + lengths_ref[doc]
        starts.append(start)
        first_start = jnp.where(start <= base, start, first_start)
        last_start = jnp.where(start < base + rows, start, last_start)
        first_finish = jnp.where(finish > base, jnp.minimum(finish, first_finish), first_finish)
        last_finish = jnp.where(finish >= base + rows, jnp.minimum(finish, last_finish), last_finish)
        start = finish
    return starts, first_start, last_start, first_finish, last_finish


def row_starts(starts, positions):
    begin = jnp.zeros_like(positions)
    for start in starts:
        begin = jnp.where(positions >= start, start, begin)
    return begin


def row_scales(starts, base, rows):
    positions = base + lax.broadcasted_iota(jnp.int32, (rows, HD), 0)
    begin = row_starts(starts, positions)
    return lax.rsqrt((positions - begin).astype(F32) + 1.0) * HD ** (-0.5)


def scale_rows(query, scales):
    heads = query.shape[1] // HD
    wide = jnp.concatenate([scales] * heads, axis=1)
    return (query.astype(F32) * wide).astype(BF16)


def dot(a, b, contract):
    return lax.dot_general(a, b, (contract, ((), ())), preferred_element_type=F32)


def states_kernel(place_ref, lengths_ref, q_ref, k_ref, v_ref, g_ref, own_ref, other_ref, gate_ref):
    rows, width = q_ref.shape
    place = place_ref[0]
    base = place * rows
    starts, _, last_start, first_finish, _ = doc_edges(lengths_ref, base, rows)
    positions = base + lax.broadcasted_iota(jnp.int32, (rows, width), 0)
    tail_keys = jnp.where(positions >= last_start, k_ref[...].astype(F32), 0.0).astype(BF16)
    tail = dot(tail_keys, v_ref[...], ((0,), (0,)))
    scaled = scale_rows(q_ref[...], row_scales(starts, base, rows)).astype(F32)
    head_rows = jnp.where(positions < first_finish, scaled, 0.0).astype(BF16)
    head = dot(head_rows, g_ref[...], ((0,), (0,)))
    odd = place % 2 == 1
    for h in range(width // HD):
        part = pl.ds(h * HD, HD)
        tail_h = tail[h * HD : (h + 1) * HD, h * HD : (h + 1) * HD]
        head_h = head[h * HD : (h + 1) * HD, h * HD : (h + 1) * HD]
        own_ref[h] = jnp.where(odd, tail_h, head_h)
        other_ref[h] = jnp.where(odd, head_h, tail_h)
    keep = jnp.where(odd, last_start < base, first_finish > base + rows)
    gate_ref[...] = jnp.full(gate_ref.shape, jnp.where(keep, 1.0, 0.0), F32)


def inner_kernel(place_ref, lengths_ref, q_ref, k_ref, v_ref, g_ref, att_ref, gq_ref, gk_ref, gv_ref):
    rows, width = q_ref.shape
    base = place_ref[0] * rows
    starts, _, _, _, _ = doc_edges(lengths_ref, base, rows)
    scaled = scale_rows(q_ref[...], row_scales(starts, base, rows))
    tile = min(256, rows)
    for at in range(0, rows, tile):
        reach = at + tile
        row_at = lax.broadcasted_iota(jnp.int32, (tile, reach), 0) + at
        column_at = lax.broadcasted_iota(jnp.int32, (tile, reach), 1)
        begin = row_starts(starts, base + row_at) - base
        allowed = (column_at <= row_at) & (column_at >= begin)
        for h in range(width // HD):
            part = slice(h * HD, (h + 1) * HD)
            scaled_t = scaled[at:reach, part]
            grad_t = g_ref[at:reach, part]
            keys = k_ref[:reach, part]
            values = v_ref[:reach, part]
            scores = dot(scaled_t, keys, ((1,), (1,)))
            weights = jnp.where(allowed, scores, 0.0).astype(BF16)
            dscores = dot(grad_t, values, ((1,), (1,)))
            dweights = jnp.where(allowed, dscores, 0.0).astype(BF16)
            att_ref[at:reach, part] = dot(weights, values, ((1,), (0,)))
            gq_ref[at:reach, part] = dot(dweights, keys, ((1,), (0,)))
            grad_k = dot(dweights, scaled_t, ((0,), (0,)))
            grad_v = dot(weights, grad_t, ((0,), (0,)))
            if at:
                gk_ref[:at, part] += grad_k[:at]
                gv_ref[:at, part] += grad_v[:at]
            gk_ref[at:reach, part] = grad_k[at:]
            gv_ref[at:reach, part] = grad_v[at:]


def split_dot(rows, state, contract):
    high = state.astype(BF16)
    low = (state - high.astype(F32)).astype(BF16)
    return dot(rows, high, contract) + dot(rows, low, contract)


def outer_kernel(slots, place_ref, lengths_ref, q_ref, k_ref, v_ref, g_ref, *refs):
    inner_refs, slot_refs, out_refs = refs[:4], refs[4 : 4 + len(slots)], refs[4 + len(slots) :]
    rows, width = q_ref.shape
    place = place_ref[0]
    base = place * rows
    starts, first_start, _, _, last_finish = doc_edges(lengths_ref, base, rows)
    odd = place % 2 == 1
    gates = []
    for steps, odd_forward in slots:
        forward = odd if odd_forward else jnp.logical_not(odd)
        before = forward & (first_start < (place - steps + 1) * rows)
        after = jnp.logical_not(forward) & (last_finish > (place + steps) * rows)
        gates.append((jnp.where(before, 1.0, 0.0), jnp.where(after, 1.0, 0.0)))
    scales = row_scales(starts, base, rows)
    scaled = scale_rows(q_ref[...], scales)
    for h in range(width // HD):
        part = slice(h * HD, (h + 1) * HD)
        entering = returning = jnp.zeros((HD, HD), F32)
        for (before, after), slot_ref in zip(gates, slot_refs):
            received = slot_ref[h]
            entering = entering + before * received
            returning = returning + after * received
        attended = inner_refs[0][:, part] + split_dot(scaled[:, part], entering, ((1,), (0,)))
        grad_q = inner_refs[1][:, part] + split_dot(g_ref[:, part], entering, ((1,), (1,)))
        grad_k = inner_refs[2][:, part] + split_dot(v_ref[:, part], returning, ((1,), (1,)))
        grad_v = inner_refs[3][:, part] + split_dot(k_ref[:, part], returning, ((1,), (0,)))
        out_refs[0][:, part] = attended.astype(BF16)
        out_refs[1][:, part] = (scales * grad_q).astype(BF16)
        out_refs[2][:, part] = grad_k.astype(BF16)
        out_refs[3][:, part] = grad_v.astype(BF16)


def body(query_rows, key_rows, value_rows, out_grad, doc_lengths):
    rows, width = query_rows.shape
    heads = width // HD
    count = lax.axis_size("ctx")
    reach = count // 4
    place = lax.axis_index("ctx").astype(jnp.int32).reshape(1)
    tensors = (query_rows, key_rows, value_rows, out_grad)
    params = pltpu.CompilerParams(vmem_limit_bytes=32 * 2**20)
    state = jax.ShapeDtypeStruct((heads, HD, HD), F32)
    own, other, gate = pl.pallas_call(
        states_kernel,
        out_shape=(state, state, jax.ShapeDtypeStruct((1, HD), F32)),
        in_specs=[SMEM, SMEM] + [VMEM] * 4,
        out_specs=[VMEM] * 3,
        compiler_params=params,
        cost_estimate=pl.CostEstimate(flops=2 * 2 * rows * width * width, bytes_accessed=4 * rows * width * 2, transcendentals=0),
        name="block_states",
    )(place, doc_lengths, *tensors)

    def send(value, pairs):
        return lax.ppermute(value, "ctx", pairs)

    mate = send(other, pair_mates(count))
    far = send(own, ring_pairs(count, reach))
    joined = own + gate[None] * mate
    slots = [(1, True), (reach, True)]
    received = [mate, far]
    for steps in range(reach - 1, 0, -1):
        pairs = swap_pairs(count, steps) if steps % 2 else ring_pairs(count, steps)
        slots.append((steps, steps % 2 == 0))
        received.append(send(joined, pairs))
    partial = jax.ShapeDtypeStruct((rows, width), F32)
    inner = pl.pallas_call(
        inner_kernel,
        out_shape=(partial,) * 4,
        in_specs=[SMEM, SMEM] + [VMEM] * 4,
        out_specs=[VMEM] * 4,
        compiler_params=params,
        cost_estimate=pl.CostEstimate(flops=6 * 2 * rows * rows * width, bytes_accessed=4 * rows * width * 6, transcendentals=0),
        name="within_block",
    )(place, doc_lengths, *tensors)
    out = jax.ShapeDtypeStruct((rows, width), BF16)
    return pl.pallas_call(
        functools.partial(outer_kernel, tuple(slots)),
        out_shape=(out,) * 4,
        in_specs=[SMEM, SMEM] + [VMEM] * (8 + len(slots)),
        out_specs=[VMEM] * 4,
        compiler_params=params,
        cost_estimate=pl.CostEstimate(flops=4 * 2 * rows * width * HD, bytes_accessed=4 * rows * width * 8, transcendentals=0),
        name="across_blocks",
    )(place, doc_lengths, *tensors, *inner, *received)


def solution(mesh):
    in_specs = (P("ctx", "head"), P("ctx", "head"), P("ctx", "head"), P("ctx", "head"), P("head"))
    out_specs = (P("ctx", "head"), P("ctx", "head"), P("ctx", "head"), P("ctx", "head"))
    return jax.shard_map(body, mesh=mesh, in_specs=in_specs, out_specs=out_specs, check_vma=False)
```

time: 96.4 us -> 29.3 us (0.30)
  the two profiles are of different devices: /device:TPU:24 before, /device:TPU:0 now
where the time goes in v1:
time: 29.3 us; the launch traced here: 29 us
  starting transfers between devices  10.5 us (36%)
  waiting for transfers between devices  7.71 us (26%)
  Pallas kernels  5.68 us (19%)
  local copies, waits for them, and re-layouts  4.45 us (15%)
  between operations  0.69 us (2%)
    ppermute x5, starting transfers between devices, send(): return lax.ppermute(value, 'ctx', pairs)  10.5 us
    ppermute x5, waiting for transfers between devices, send(): return lax.ppermute(value, 'ctx', pairs)  7.71 us
    unnamed x10, local copies, waits for them, and re-layouts  4.45 us
    pallas_call x1, Pallas kernels, body(): pl.pallas_call(inner_kernel, out_shape=(partial,) * 4, in_specs=[SMEM, SM...  2.37 us
    pallas_call x1, Pallas kernels, body(): pl.pallas_call(functools.partial(outer_kernel, tuple(slots)), out_shape=(...  2.22 us
    pallas_call x1, Pallas kernels, body(): pl.pallas_call(states_kernel, out_shape=(state, state, jax.ShapeDtypeStru...  1.09 us
  transfers between devices with their start and end apart: 5, of which 3 were waited for; matrix products, arithmetic and copies ran while one was open for 0% of the time, Pallas kernels for 8%

profile of v1, /device:TPU:0, one launch (start us, length us, event | category | flops | bytes accessed | tf_op | source)
XLA Modules:
  0.0 29.0 jit_solution(18367608686048345256)
XLA Ops:
  0.6 0.0 copy-start.4
  0.6 0.6 %copy-done.4 = s32[8]{0:T(128)S(1)} copy-done((s32[8]{0:T(128)S(1)}, s32[8]{0:T(128)}, u32[]{:S(2)}) %copy-start.4) | copy-done | bytes 56
  1.3 0.0 copy-start
  1.3 0.9 %copy-done = bf16[512,256]{1,0:T(8,128)(2,1)S(1)} copy-done((bf16[512,256]{1,0:T(8,128)(2,1)S(1)}, bf16[512,256]{1,0:T(8,128)(2,1)}, u32[]{:S(2)}) %copy-start) | copy-done | bytes 262168
  2.2 0.0 copy-start.1
  2.2 0.9 %copy-done.1 = bf16[512,256]{1,0:T(8,128)(2,1)S(1)} copy-done((bf16[512,256]{1,0:T(8,128)(2,1)S(1)}, bf16[512,256]{1,0:T(8,128)(2,1)}, u32[]{:S(2)}) %copy-start.1) | copy-done | bytes 262168
  3.2 0.0 copy-start.2
  3.2 0.9 %copy-done.2 = bf16[512,256]{1,0:T(8,128)(2,1)S(1)} copy-done((bf16[512,256]{1,0:T(8,128)(2,1)S(1)}, bf16[512,256]{1,0:T(8,128)(2,1)}, u32[]{:S(2)}) %copy-start.2) | copy-done | bytes 262168
  4.1 0.0 copy-start.3
  4.1 0.9 %copy-done.3 = bf16[512,256]{1,0:T(8,128)(2,1)S(1)} copy-done((bf16[512,256]{1,0:T(8,128)(2,1)S(1)}, bf16[512,256]{1,0:T(8,128)(2,1)}, u32[]{:S(2)}) %copy-start.3) | copy-done | bytes 262168
  5.1 1.1 %block_states.1 = (f32[2,128,128]{2,1,0:T(8,128)S(1)}, f32[2,128,128]{2,1,0:T(8,128)S(1)}, f32[1,128]{1,0:T(1,128)S(1)}) custom-call(s32[1]{0:T(128)} %bitcast.place_ref, s32[8]{0:T(128)S(1)} %copy-done.4, bf16[512,256]{1,0:T(8,128)(2,1)S(1)} %copy-done, bf16[512,256]{1,0:T(8,128)(2,1)S(1)} %copy-done.1, bf16[512,256]{1,0:T(8,128)(2,1)S(1)} %copy-done.2, ...), custom_call_target="tpu_custom_call" | custom-call | flops 134217728 | bytes 1048576 | tf_op jit(solution)/shard_map/block_states/pallas_call | solution.py:187
  6.2 3.0 %collective-permute-start = (f32[2,128,128]{2,1,0:T(8,128)S(1)}, f32[2,128,128]{2,1,0:T(8,128)S(1)}, u32[]{:S(2)}, u32[]{:S(2)}) collective-permute-start(f32[2,128,128]{2,1,0:T(8,128)S(1)} %get-tuple-element.15), channel_id=1, source_target_pairs={{0,2},{2,0},{4,6},{6,4},{8,10},{10,8},{12,14},{14,12},{16,18},{18,... | collective-permute-start | bytes 393224 | tf_op jit(solution)/shard_map/ppermute | solution.py:198
  9.2 0.1 collective-permute-start.1
  9.3 3.8 %collective-permute-done.refs_4_ = f32[2,128,128]{2,1,0:T(8,128)S(1)} collective-permute-done((f32[2,128,128]{2,1,0:T(8,128)S(1)}, f32[2,128,128]{2,1,0:T(8,128)S(1)}, u32[]{:S(2)}, u32[]{:S(2)}) %collective-permute-start) | collective-permute-done | bytes 131104 | tf_op jit(solution)/shard_map/ppermute | solution.py:198
  13.1 5.4 %collective-permute-start.4 = (f32[2,128,128]{2,1,0:T(8,128)S(1)}, f32[2,128,128]{2,1,0:T(8,128)S(1)}, u32[]{:S(2)}, u32[]{:S(2)}) collective-permute-start(f32[2,128,128]{2,1,0:T(8,128)S(1)} %multiply_add_fusion), channel_id=1, source_target_pairs={{2,4},{6,8},{10,12},{14,16},{18,20},{22,24},{26,28},{4,2},{8,6},{1... | collective-permute-start | bytes 393224 | tf_op jit(solution)/shard_map/ppermute | solution.py:198
  18.5 0.0 collective-permute-start.3
  18.5 2.0 %collective-permute-start.2 = (f32[2,128,128]{2,1,0:T(8,128)S(1)}, f32[2,128,128]{2,1,0:T(8,128)S(1)}, u32[]{:S(2)}, u32[]{:S(2)}) collective-permute-start(f32[2,128,128]{2,1,0:T(8,128)S(1)} %multiply_add_fusion), channel_id=1, source_target_pairs={{2,8},{6,12},{10,16},{14,20},{18,24},{22,28},{8,2},{12,6},{16,10},... | collective-permute-start | bytes 393224 | tf_op jit(solution)/shard_map/ppermute | solution.py:198
  20.5 2.4 %within_block.1 = (f32[512,256]{1,0:T(8,128)S(1)}, f32[512,256]{1,0:T(8,128)S(1)}, f32[512,256]{1,0:T(8,128)S(1)}, f32[512,256]{1,0:T(8,128)S(1)}) custom-call(s32[1]{0:T(128)} %bitcast.place_ref, s32[8]{0:T(128)S(1)} %copy-done.4, bf16[512,256]{1,0:T(8,128)(2,1)S(1)} %copy-done, bf16[512,256]{1,0:T(8,128)(2,1)S(1)} %copy-done.1, ...), custom_call_target="tpu_custom_call" | custom-call | flops 805306368 | bytes 3145728 | tf_op jit(solution)/shard_map/within_block/pallas_call | solution.py:210
  22.9 0.0 collective-permute-done.1.refs_5_
  22.9 0.0 collective-permute-done.4.refs_8_
  22.9 2.0 %collective-permute-done.3.refs_7_ = f32[2,128,128]{2,1,0:T(8,128)S(1)} collective-permute-done((f32[2,128,128]{2,1,0:T(8,128)S(1)}, f32[2,128,128]{2,1,0:T(8,128)S(1)}, u32[]{:S(2)}, u32[]{:S(2)}) %collective-permute-start.3) | collective-permute-done | bytes 131104 | tf_op jit(solution)/shard_map/ppermute | solution.py:198
  25.0 1.9 %collective-permute-done.2.refs_6_ = f32[2,128,128]{2,1,0:T(8,128)S(1)} collective-permute-done((f32[2,128,128]{2,1,0:T(8,128)S(1)}, f32[2,128,128]{2,1,0:T(8,128)S(1)}, u32[]{:S(2)}, u32[]{:S(2)}) %collective-permute-start.2) | collective-permute-done | bytes 131104 | tf_op jit(solution)/shard_map/ppermute | solution.py:198
  26.8 2.2 %across_blocks.1 = (bf16[512,256]{1,0:T(8,128)(2,1)}, bf16[512,256]{1,0:T(8,128)(2,1)}, bf16[512,256]{1,0:T(8,128)(2,1)}, bf16[512,256]{1,0:T(8,128)(2,1)}) custom-call(s32[1]{0:T(128)} %bitcast.place_ref, s32[8]{0:T(128)S(1)} %copy-done.4, bf16[512,256]{1,0:T(8,128)(2,1)S(1)} %copy-done, bf16[512,256]{1,0:T(8,128)(2,1)S(1)} %copy-done.1, ...), custom_call_target="tpu_custom_call" | custom-call | flops 134217728 | bytes 4194304 | tf_op jit(solution)/shard_map/across_blocks/pallas_call | solution.py:220
  (1 shorter events, 0.0 us)
Async XLA Ops:
  0.6 0.7 %copy-start.4 = (s32[8]{0:T(128)S(1)}, s32[8]{0:T(128)}, u32[]{:S(2)}) copy-start(s32[8]{0:T(128)} %lengths_ref.5) | copy-start | bytes 100
  1.3 0.9 %copy-start = (bf16[512,256]{1,0:T(8,128)(2,1)S(1)}, bf16[512,256]{1,0:T(8,128)(2,1)}, u32[]{:S(2)}) copy-start(bf16[512,256]{1,0:T(8,128)(2,1)} %q_ref.5) | copy-start | bytes 786436
  2.2 0.9 %copy-start.1 = (bf16[512,256]{1,0:T(8,128)(2,1)S(1)}, bf16[512,256]{1,0:T(8,128)(2,1)}, u32[]{:S(2)}) copy-start(bf16[512,256]{1,0:T(8,128)(2,1)} %k_ref.5) | copy-start | bytes 786436
  3.2 0.9 %copy-start.2 = (bf16[512,256]{1,0:T(8,128)(2,1)S(1)}, bf16[512,256]{1,0:T(8,128)(2,1)}, u32[]{:S(2)}) copy-start(bf16[512,256]{1,0:T(8,128)(2,1)} %v_ref.5) | copy-start | bytes 786436
  4.1 0.9 %copy-start.3 = (bf16[512,256]{1,0:T(8,128)(2,1)S(1)}, bf16[512,256]{1,0:T(8,128)(2,1)}, u32[]{:S(2)}) copy-start(bf16[512,256]{1,0:T(8,128)(2,1)} %g_ref.5) | copy-start | bytes 786436
  6.2 6.9 %collective-permute-start = (f32[2,128,128]{2,1,0:T(8,128)S(1)}, f32[2,128,128]{2,1,0:T(8,128)S(1)}, u32[]{:S(2)}, u32[]{:S(2)}) collective-permute-start(f32[2,128,128]{2,1,0:T(8,128)S(1)} %get-tuple-element.15), channel_id=1, source_target_pairs={{0,2},{2,0},{4,6},{6,4},{8,10},{10,8},{12,14},{14,12},{16,18},{18,... | collective-permute-start | bytes 393224 | tf_op jit(solution)/shard_map/ppermute | solution.py:198
  9.2 13.7 %collective-permute-start.1 = (f32[2,128,128]{2,1,0:T(8,128)S(1)}, f32[2,128,128]{2,1,0:T(8,128)S(1)}, u32[]{:S(2)}, u32[]{:S(2)}) collective-permute-start(f32[2,128,128]{2,1,0:T(8,128)S(1)} %get-tuple-element.16), channel_id=1, source_target_pairs={{0,2},{2,10},{4,6},{6,14},{8,0},{10,18},{12,4},{14,22},{16,8},{18,... | collective-permute-start | bytes 393224 | tf_op jit(solution)/shard_map/ppermute | solution.py:198
  13.1 9.8 %collective-permute-start.4 = (f32[2,128,128]{2,1,0:T(8,128)S(1)}, f32[2,128,128]{2,1,0:T(8,128)S(1)}, u32[]{:S(2)}, u32[]{:S(2)}) collective-permute-start(f32[2,128,128]{2,1,0:T(8,128)S(1)} %multiply_add_fusion), channel_id=1, source_target_pairs={{2,4},{6,8},{10,12},{14,16},{18,20},{22,24},{26,28},{4,2},{8,6},{1... | collective-permute-start | bytes 393224 | tf_op jit(solution)/shard_map/ppermute | solution.py:198
  18.5 6.4 %collective-permute-start.3 = (f32[2,128,128]{2,1,0:T(8,128)S(1)}, f32[2,128,128]{2,1,0:T(8,128)S(1)}, u32[]{:S(2)}, u32[]{:S(2)}) collective-permute-start(f32[2,128,128]{2,1,0:T(8,128)S(1)} %multiply_add_fusion), channel_id=1, source_target_pairs={{0,2},{2,6},{4,0},{6,10},{8,4},{10,14},{12,8},{14,18},{16,12},{18,... | collective-permute-start | bytes 393224 | tf_op jit(solution)/shard_map/ppermute | solution.py:198
  18.5 8.3 %collective-permute-start.2 = (f32[2,128,128]{2,1,0:T(8,128)S(1)}, f32[2,128,128]{2,1,0:T(8,128)S(1)}, u32[]{:S(2)}, u32[]{:S(2)}) collective-permute-start(f32[2,128,128]{2,1,0:T(8,128)S(1)} %multiply_add_fusion), channel_id=1, source_target_pairs={{2,8},{6,12},{10,16},{14,20},{18,24},{22,28},{8,2},{12,6},{16,10},... | collective-permute-start | bytes 393224 | tf_op jit(solution)/shard_map/ppermute | solution.py:198

commit v2 on v1

v2 whole, which is shorter than its diff:
```python
import functools

import jax
import jax.numpy as jnp
from jax import lax
from jax.experimental import pallas as pl
from jax.experimental.pallas import tpu as pltpu
from jax.sharding import PartitionSpec as P

HD = 128
F32 = jnp.float32
BF16 = jnp.bfloat16
HBM = pl.BlockSpec(memory_space=pltpu.HBM)
VMEM = pl.BlockSpec(memory_space=pltpu.VMEM)


def cycle_within(nodes):
    return [(node, nodes[(at + 1) % len(nodes)]) for at, node in enumerate(nodes)]


def swap_pairs(count, steps):
    pairs = [(j, j + steps) for j in range(1, count - steps, 2)]
    met = {j for pair in pairs for j in pair}
    rest = [j for j in range(count) if j not in met]
    low = [j for j in rest if j < count // 2]
    high = [j for j in rest if j >= count // 2]
    groups = [low, high] if len(low) != 1 and len(high) != 1 else [rest]
    fill = [edge for group in groups for edge in cycle_within(group)]
    return pairs + [(b, a) for a, b in pairs] + fill


def ring_pairs(count, steps):
    out = []
    for j in range(count):
        target = j + steps if j % 2 else j - steps
        if not 0 <= target < count:
            target = j - 1 if j % 2 else j + 1
        out.append((j, target))
    return out


def pair_mates(count):
    return [(j, j ^ 1) for j in range(count)]


def doc_edges(lengths_ref, base, rows):
    first_start = last_start = jnp.int32(0)
    first_finish = last_finish = jnp.int32(2**30)
    start = jnp.int32(0)
    starts = []
    for doc in range(lengths_ref.shape[0]):
        finish = start + lengths_ref[doc]
        starts.append(start)
        first_start = jnp.where(start <= base, start, first_start)
        last_start = jnp.where(start < base + rows, start, last_start)
        first_finish = jnp.where(finish > base, jnp.minimum(finish, first_finish), first_finish)
        last_finish = jnp.where(finish >= base + rows, jnp.minimum(finish, last_finish), last_finish)
        start = finish
    return starts, first_start, last_start, first_finish, last_finish


def row_begins(starts, base, rows):
    local = lax.broadcasted_iota(jnp.int32, (rows, HD), 0)
    begin = jnp.full((rows, HD), -base, jnp.int32)
    for start in starts:
        begin = jnp.where(local >= start - base, start - base, begin)
    return begin


def row_scales(begin):
    local = lax.broadcasted_iota(jnp.int32, begin.shape, 0)
    return lax.rsqrt((local - begin).astype(F32) + 1.0) * HD ** (-0.5)


def scale_rows(query, scales):
    heads = query.shape[1] // HD
    wide = jnp.concatenate([scales] * heads, axis=1)
    return (query.astype(F32) * wide).astype(BF16)


def dot(a, b, contract):
    return lax.dot_general(a, b, (contract, ((), ())), preferred_element_type=F32)


def states_kernel(
    lengths_hbm, q_hbm, k_hbm, v_hbm, g_hbm,
    own_ref, other_ref, gate_ref, begin_ref, scaled_ref, k_ref, v_ref, g_ref,
    q_ref, lengths_ref, sems,
):
    pieces = [(lengths_hbm, lengths_ref), (k_hbm, k_ref), (v_hbm, v_ref), (q_hbm, q_ref), (g_hbm, g_ref)]
    copies = [pltpu.make_async_copy(source, target, sems.at[at]) for at, (source, target) in enumerate(pieces)]
    for copy in copies:
        copy.start()
    rows, width = q_ref.shape
    place = lax.axis_index("ctx")
    base = place * rows
    copies[0].wait()
    starts, _, last_start, first_finish, _ = doc_edges(lengths_ref, base, rows)
    odd = place % 2 == 1
    keep = jnp.where(odd, last_start < base, first_finish > base + rows)
    gate_ref[...] = jnp.full(gate_ref.shape, jnp.where(keep, 1.0, 0.0), F32)
    begin = row_begins(starts, base, rows)
    begin_ref[...] = begin
    scales = row_scales(begin)
    local = lax.broadcasted_iota(jnp.int32, (rows, width), 0)
    copies[1].wait()
    tail_keys = jnp.where(local >= last_start - base, k_ref[...].astype(F32), 0.0).astype(BF16)
    copies[2].wait()
    tail = dot(tail_keys, v_ref[...], ((0,), (0,)))
    copies[3].wait()
    scaled = scale_rows(q_ref[...], scales)
    scaled_ref[...] = scaled
    head_rows = jnp.where(local < first_finish - base, scaled.astype(F32), 0.0).astype(BF16)
    copies[4].wait()
    head = dot(head_rows, g_ref[...], ((0,), (0,)))
    for h in range(width // HD):
        part = slice(h * HD, (h + 1) * HD)
        own_ref[h] = jnp.where(odd, tail[part, part], head[part, part])
        other_ref[h] = jnp.where(odd, head[part, part], tail[part, part])


def inner_kernel(
    slots, lengths_hbm, begin_ref, scaled_ref, k_ref, v_ref, g_ref,
    gates_ref, att_ref, gq_ref, gk_ref, gv_ref, lengths_ref, sem,
):
    copy = pltpu.make_async_copy(lengths_hbm, lengths_ref, sem)
    copy.start()
    rows, width = scaled_ref.shape
    copy.wait()
    place = lax.axis_index("ctx")
    base = place * rows
    _, first_start, _, _, last_finish = doc_edges(lengths_ref, base, rows)
    odd = place % 2 == 1
    gates = []
    for steps, odd_forward in slots:
        forward = odd if odd_forward else jnp.logical_not(odd)
        gates.append(forward & (first_start < (place - steps + 1) * rows))
        gates.append(jnp.logical_not(forward) & (last_finish > (place + steps) * rows))
    for at, gate in enumerate(gates):
        gates_ref[at : at + 1, :] = jnp.full((1, HD), jnp.where(gate, 1.0, 0.0), F32)
    tile = min(256, rows)
    for at in range(0, rows, tile):
        reach = at + tile
        row_at = lax.broadcasted_iota(jnp.int32, (tile, reach), 0) + at
        column_at = lax.broadcasted_iota(jnp.int32, (tile, reach), 1)
        begin = jnp.concatenate([begin_ref[at:reach, :]] * (reach // HD), axis=1)
        allowed = (column_at <= row_at) & (column_at >= begin)
        for h in range(width // HD):
            part = slice(h * HD, (h + 1) * HD)
            scaled_t = scaled_ref[at:reach, part]
            grad_t = g_ref[at:reach, part]
            keys = k_ref[:reach, part]
            values = v_ref[:reach, part]
            scores = dot(scaled_t, keys, ((1,), (1,)))
            weights = jnp.where(allowed, scores, 0.0).astype(BF16)
            dscores = dot(grad_t, values, ((1,), (1,)))
            dweights = jnp.where(allowed, dscores, 0.0).astype(BF16)
            att_ref[at:reach, part] = dot(weights, values, ((1,), (0,)))
            gq_ref[at:reach, part] = dot(dweights, keys, ((1,), (0,)))
            grad_k = dot(dweights, scaled_t, ((0,), (0,)))
            grad_v = dot(weights, grad_t, ((0,), (0,)))
            if at:
                gk_ref[:at, part] += grad_k[:at]
                gv_ref[:at, part] += grad_v[:at]
            gk_ref[at:reach, part] = grad_k[at:]
            gv_ref[at:reach, part] = grad_v[at:]


def diagonal(blocks):
    zero = jnp.zeros((HD, HD), BF16)
    rows = [
        jnp.concatenate([block.astype(BF16) if h == at else zero for h in range(len(blocks))], axis=1)
        for at, block in enumerate(blocks)
    ]
    return jnp.concatenate(rows, axis=0)


def split(blocks):
    low = [block - block.astype(BF16).astype(F32) for block in blocks]
    return diagonal(blocks), diagonal(low)


def split_dot(rows, state, contract):
    return dot(rows, state[0], contract) + dot(rows, state[1], contract)


def outer_kernel(begin_ref, scaled_ref, k_ref, v_ref, g_ref, gates_ref, *refs):
    out_hbms, out_refs, sems = refs[-9:-5], refs[-5:-1], refs[-1]
    inner_refs, slot_refs = refs[:4], refs[4:-9]
    heads = scaled_ref.shape[1] // HD
    entering = [jnp.zeros((HD, HD), F32)] * heads
    returning = [jnp.zeros((HD, HD), F32)] * heads
    for at, slot_ref in enumerate(slot_refs):
        before, after = gates_ref[2 * at : 2 * at + 1, :], gates_ref[2 * at + 1 : 2 * at + 2, :]
        entering = [state + before * slot_ref[h] for h, state in enumerate(entering)]
        returning = [state + after * slot_ref[h] for h, state in enumerate(returning)]
    entering, returning = split(entering), split(returning)
    copies = [pltpu.make_async_copy(out_refs[at], out_hbms[at], sems.at[at]) for at in range(4)]
    attended = inner_refs[0][...] + split_dot(scaled_ref[...], entering, ((1,), (0,)))
    out_refs[0][...] = attended.astype(BF16)
    copies[0].start()
    scales = jnp.concatenate([row_scales(begin_ref[...])] * heads, axis=1)
    grad_q = inner_refs[1][...] + split_dot(g_ref[...], entering, ((1,), (1,)))
    out_refs[1][...] = (scales * grad_q).astype(BF16)
    copies[1].start()
    grad_k = inner_refs[2][...] + split_dot(v_ref[...], returning, ((1,), (1,)))
    out_refs[2][...] = grad_k.astype(BF16)
    copies[2].start()
    grad_v = inner_refs[3][...] + split_dot(k_ref[...], returning, ((1,), (0,)))
    out_refs[3][...] = grad_v.astype(BF16)
    copies[3].start()
    for copy in copies:
        copy.wait()


def body(query_rows, key_rows, value_rows, out_grad, doc_lengths):
    rows, width = query_rows.shape
    heads = width // HD
    docs = doc_lengths.shape[0]
    count = lax.axis_size("ctx")
    reach = count // 4
    arguments = (doc_lengths, query_rows, key_rows, value_rows, out_grad)
    held = [pltpu.with_memory_space_constraint(x, pltpu.HBM) for x in arguments]
    params = pltpu.CompilerParams(vmem_limit_bytes=32 * 2**20)
    state = jax.ShapeDtypeStruct((heads, HD, HD), F32)
    flat = jax.ShapeDtypeStruct((rows, width), BF16)
    partial = jax.ShapeDtypeStruct((rows, width), F32)
    own, other, gate, begin, *tensors = pl.pallas_call(
        states_kernel,
        out_shape=(state, state, jax.ShapeDtypeStruct((1, HD), F32), jax.ShapeDtypeStruct((rows, HD), jnp.int32)) + (flat,) * 4,
        in_specs=[HBM] * 5,
        out_specs=[VMEM] * 8,
        scratch_shapes=[pltpu.VMEM((rows, width), BF16), pltpu.SMEM((docs,), jnp.int32), pltpu.SemaphoreType.DMA((5,))],
        compiler_params=params,
        cost_estimate=pl.CostEstimate(flops=2 * 2 * rows * width * width, bytes_accessed=4 * rows * width * 2, transcendentals=0),
        name="block_states",
    )(*held)

    def send(value, pairs):
        return lax.ppermute(value, "ctx", pairs)

    mate = send(other, pair_mates(count))
    far = send(own, ring_pairs(count, reach))
    joined = own + gate[None] * mate
    slots = [(1, True), (reach, True)]
    received = [mate, far]
    for steps in range(1, reach):
        pairs = swap_pairs(count, steps) if steps % 2 else ring_pairs(count, steps)
        slots.append((steps, steps % 2 == 0))
        received.append(send(joined, pairs))
    inner = pl.pallas_call(
        functools.partial(inner_kernel, tuple(slots)),
        out_shape=(jax.ShapeDtypeStruct((2 * len(slots), HD), F32),) + (partial,) * 4,
        in_specs=[HBM] + [VMEM] * 5,
        out_specs=[VMEM] * 5,
        scratch_shapes=[pltpu.SMEM((docs,), jnp.int32), pltpu.SemaphoreType.DMA(())],
        compiler_params=params,
        cost_estimate=pl.CostEstimate(flops=6 * 2 * rows * rows * width, bytes_accessed=4 * rows * width * 6, transcendentals=0),
        name="within_block",
    )(held[0], begin, *tensors)
    return pl.pallas_call(
        outer_kernel,
        out_shape=(flat,) * 4,
        in_specs=[VMEM] * (10 + len(slots)),
        out_specs=[HBM] * 4,
        scratch_shapes=[pltpu.VMEM((rows, width), BF16)] * 4 + [pltpu.SemaphoreType.DMA((4,))],
        compiler_params=params,
        cost_estimate=pl.CostEstimate(flops=4 * 2 * rows * width * HD, bytes_accessed=4 * rows * width * 8, transcendentals=0),
        name="across_blocks",
    )(begin, *tensors, *inner, *received)


def solution(mesh):
    in_specs = (P("ctx", "head"), P("ctx", "head"), P("ctx", "head"), P("ctx", "head"), P("head"))
    out_specs = (P("ctx", "head"), P("ctx", "head"), P("ctx", "head"), P("ctx", "head"))
    return jax.shard_map(body, mesh=mesh, in_specs=in_specs, out_specs=out_specs, check_vma=False)
```

time: 29.3 us -> 22.6 us (0.77)
  local copies, waits for them, and re-layouts: 4.45 us -> 0 us
  waiting for transfers between devices: 7.71 us -> 5.51 us
    unnamed x10 -> x0, local copies, waits for them, and re-layouts: 4.45 us -> none
    ppermute x5, waiting for transfers between devices: 7.71 us -> 5.51 us  [send(): return lax.ppermute(value, 'ctx', pairs)]
    pallas_call x1, Pallas kernels: 1.09 us -> 1.81 us  [body(): pl.pallas_call(states_kernel, out_shape=(state, state, jax.ShapeDtypeStru...]
    pallas_call x2, Pallas kernels: 4.59 us -> 4.08 us  [the longest x1 2.5 us: body(): pl.pallas_call(functools.partial(inner_kernel, tuple(slots)), out_shape=(...]
  transfers between devices with their start and end apart: 5 -> 5, of which waited for: 3 -> 2; matrix products, arithmetic and copies ran while one was open for 0% -> 0% of each run, Pallas kernels for 8% -> 11%
where the time goes in v2:
time: 22.6 us; the launch traced here: 22.5 us
  starting transfers between devices  10.4 us (46%)
  Pallas kernels  5.89 us (26%)
  waiting for transfers between devices  5.51 us (24%)
  between operations  0.68 us (3%)
    ppermute x5, starting transfers between devices, send(): return lax.ppermute(value, 'ctx', pairs)  10.4 us
    ppermute x5, waiting for transfers between devices, send(): return lax.ppermute(value, 'ctx', pairs)  5.51 us
    pallas_call x1, Pallas kernels, body(): pl.pallas_call(functools.partial(inner_kernel, tuple(slots)), out_shape=(...  2.5 us
    pallas_call x1, Pallas kernels, body(): pl.pallas_call(states_kernel, out_shape=(state, state, jax.ShapeDtypeStru...  1.81 us
    pallas_call x1, Pallas kernels, body(): pl.pallas_call(outer_kernel, out_shape=(flat,) * 4, in_specs=[VMEM] * (10...  1.58 us
  transfers between devices with their start and end apart: 5, of which 2 were waited for; matrix products, arithmetic and copies ran while one was open for 0% of the time, Pallas kernels for 11%

profile of v2, /device:TPU:0, one launch (start us, length us, event | category | flops | bytes accessed | tf_op | source)
XLA Modules:
  0.0 22.5 jit_solution(12233724182911405257)
XLA Ops:
  0.6 1.8 %block_states.1 = (f32[2,128,128]{2,1,0:T(8,128)S(1)}, f32[2,128,128]{2,1,0:T(8,128)S(1)}, f32[1,128]{1,0:T(1,128)S(1)}, s32[512,128]{1,0:T(8,128)S(1)}, bf16[51...) custom-call(s32[8]{0:T(128)} %lengths_hbm.3, ...), custom_call_target="tpu_custom_call" | custom-call | flops 134217728 | bytes 1048576 | tf_op jit(solution)/shard_map/block_states/pallas_call | solution.py:228
  2.4 3.0 %collective-permute-start = (f32[2,128,128]{2,1,0:T(8,128)S(1)}, f32[2,128,128]{2,1,0:T(8,128)S(1)}, u32[]{:S(2)}, u32[]{:S(2)}) collective-permute-start(f32[2,128,128]{2,1,0:T(8,128)S(1)} %get-tuple-element.27), channel_id=1, source_target_pairs={{0,2},{2,0},{4,6},{6,4},{8,10},{10,8},{12,14},{14,12},{16,18},{18,... | collective-permute-start | bytes 393224 | tf_op jit(solution)/shard_map/ppermute | solution.py:240
  5.4 0.1 collective-permute-start.1
  5.5 3.8 %collective-permute-done.refs_4_ = f32[2,128,128]{2,1,0:T(8,128)S(1)} collective-permute-done((f32[2,128,128]{2,1,0:T(8,128)S(1)}, f32[2,128,128]{2,1,0:T(8,128)S(1)}, u32[]{:S(2)}, u32[]{:S(2)}) %collective-permute-start) | collective-permute-done | bytes 131104 | tf_op jit(solution)/shard_map/ppermute | solution.py:240
  9.4 1.6 %collective-permute-start.4 = (f32[2,128,128]{2,1,0:T(8,128)S(1)}, f32[2,128,128]{2,1,0:T(8,128)S(1)}, u32[]{:S(2)}, u32[]{:S(2)}) collective-permute-start(f32[2,128,128]{2,1,0:T(8,128)S(1)} %multiply_add_fusion), channel_id=1, source_target_pairs={{2,8},{6,12},{10,16},{14,20},{18,24},{22,28},{8,2},{12,6},{16,10},... | collective-permute-start | bytes 393224 | tf_op jit(solution)/shard_map/ppermute | solution.py:240
  11.0 1.4 %collective-permute-start.3 = (f32[2,128,128]{2,1,0:T(8,128)S(1)}, f32[2,128,128]{2,1,0:T(8,128)S(1)}, u32[]{:S(2)}, u32[]{:S(2)}) collective-permute-start(f32[2,128,128]{2,1,0:T(8,128)S(1)} %multiply_add_fusion), channel_id=1, source_target_pairs={{0,2},{2,6},{4,0},{6,10},{8,4},{10,14},{12,8},{14,18},{16,12},{18,... | collective-permute-start | bytes 393224 | tf_op jit(solution)/shard_map/ppermute | solution.py:240
  12.3 4.4 %collective-permute-start.2 = (f32[2,128,128]{2,1,0:T(8,128)S(1)}, f32[2,128,128]{2,1,0:T(8,128)S(1)}, u32[]{:S(2)}, u32[]{:S(2)}) collective-permute-start(f32[2,128,128]{2,1,0:T(8,128)S(1)} %multiply_add_fusion), channel_id=1, source_target_pairs={{2,4},{6,8},{10,12},{14,16},{18,20},{22,24},{26,28},{4,2},{8,6},{1... | collective-permute-start | bytes 393224 | tf_op jit(solution)/shard_map/ppermute | solution.py:240
  16.7 2.5 %within_block.1 = (f32[10,128]{1,0:T(8,128)S(1)}, f32[512,256]{1,0:T(8,128)S(1)}, f32[512,256]{1,0:T(8,128)S(1)}, f32[512,256]{1,0:T(8,128)S(1)}, f32[512,256]{1,0:T(8,128)S(1)}) custom-call(s32[8]{0:T(128)} %lengths_hbm.3, s32[512,128]{1,0:T(8,128)S(1)} %get-tuple-element.17.begin_ref, bf16[512,256]{1,0:T(8,128)(2,1)S(1)} %get-tuple-element.18.scaled_ref, ...), custom_call_target="tpu_custom_call" | custom-call | flops 805306368 | bytes 3145728 | tf_op jit(solution)/shard_map/within_block/pallas_call | solution.py:251
  19.2 0.0 collective-permute-done.1.refs_5_
  19.2 0.0 collective-permute-done.4.refs_8_
  19.2 0.0 collective-permute-done.3.refs_7_
  19.2 1.7 %collective-permute-done.2.refs_6_ = f32[2,128,128]{2,1,0:T(8,128)S(1)} collective-permute-done((f32[2,128,128]{2,1,0:T(8,128)S(1)}, f32[2,128,128]{2,1,0:T(8,128)S(1)}, u32[]{:S(2)}, u32[]{:S(2)}) %collective-permute-start.2) | collective-permute-done | bytes 131104 | tf_op jit(solution)/shard_map/ppermute | solution.py:240
  20.9 1.6 %across_blocks.1 = (bf16[512,256]{1,0:T(8,128)(2,1)}, bf16[512,256]{1,0:T(8,128)(2,1)}, bf16[512,256]{1,0:T(8,128)(2,1)}, bf16[512,256]{1,0:T(8,128)(2,1)}) custom-call(s32[512,128]{1,0:T(8,128)S(1)} %get-tuple-element.17.begin_ref, bf16[512,256]{1,0:T(8,128)(2,1)S(1)} %get-tuple-element.18.scaled_ref, bf16[512,256]{1,0:T(8,128)(2,1)S(1)} %get-tuple-element.19.k_ref, ...), custom_call_target="tpu_custom_call" | custom-call | flops 134217728 | bytes 4194304 | tf_op jit(solution)/shard_map/across_blocks/pallas_call | solution.py:261
  (1 shorter events, 0.0 us)
Async XLA Ops:
  2.4 6.9 %collective-permute-start = (f32[2,128,128]{2,1,0:T(8,128)S(1)}, f32[2,128,128]{2,1,0:T(8,128)S(1)}, u32[]{:S(2)}, u32[]{:S(2)}) collective-permute-start(f32[2,128,128]{2,1,0:T(8,128)S(1)} %get-tuple-element.27), channel_id=1, source_target_pairs={{0,2},{2,0},{4,6},{6,4},{8,10},{10,8},{12,14},{14,12},{16,18},{18,... | collective-permute-start | bytes 393224 | tf_op jit(solution)/shard_map/ppermute | solution.py:240
  5.4 13.7 %collective-permute-start.1 = (f32[2,128,128]{2,1,0:T(8,128)S(1)}, f32[2,128,128]{2,1,0:T(8,128)S(1)}, u32[]{:S(2)}, u32[]{:S(2)}) collective-permute-start(f32[2,128,128]{2,1,0:T(8,128)S(1)} %get-tuple-element.28), channel_id=1, source_target_pairs={{0,2},{2,10},{4,6},{6,14},{8,0},{10,18},{12,4},{14,22},{16,8},{18,... | collective-permute-start | bytes 393224 | tf_op jit(solution)/shard_map/ppermute | solution.py:240
  9.4 9.8 %collective-permute-start.4 = (f32[2,128,128]{2,1,0:T(8,128)S(1)}, f32[2,128,128]{2,1,0:T(8,128)S(1)}, u32[]{:S(2)}, u32[]{:S(2)}) collective-permute-start(f32[2,128,128]{2,1,0:T(8,128)S(1)} %multiply_add_fusion), channel_id=1, source_target_pairs={{2,8},{6,12},{10,16},{14,20},{18,24},{22,28},{8,2},{12,6},{16,10},... | collective-permute-start | bytes 393224 | tf_op jit(solution)/shard_map/ppermute | solution.py:240
  11.0 8.3 %collective-permute-start.3 = (f32[2,128,128]{2,1,0:T(8,128)S(1)}, f32[2,128,128]{2,1,0:T(8,128)S(1)}, u32[]{:S(2)}, u32[]{:S(2)}) collective-permute-start(f32[2,128,128]{2,1,0:T(8,128)S(1)} %multiply_add_fusion), channel_id=1, source_target_pairs={{0,2},{2,6},{4,0},{6,10},{8,4},{10,14},{12,8},{14,18},{16,12},{18,... | collective-permute-start | bytes 393224 | tf_op jit(solution)/shard_map/ppermute | solution.py:240
  12.3 8.6 %collective-permute-start.2 = (f32[2,128,128]{2,1,0:T(8,128)S(1)}, f32[2,128,128]{2,1,0:T(8,128)S(1)}, u32[]{:S(2)}, u32[]{:S(2)}) collective-permute-start(f32[2,128,128]{2,1,0:T(8,128)S(1)} %multiply_add_fusion), channel_id=1, source_target_pairs={{2,4},{6,8},{10,12},{14,16},{18,20},{22,24},{26,28},{4,2},{8,6},{1... | collective-permute-start | bytes 393224 | tf_op jit(solution)/shard_map/ppermute | solution.py:240

commit v3 on v2

--- a/solution.py
+++ b/solution.py
@@ -14,33 +14,32 @@
 VMEM = pl.BlockSpec(memory_space=pltpu.VMEM)
 
 
-def cycle_within(nodes):
-    return [(node, nodes[(at + 1) % len(nodes)]) for at, node in enumerate(nodes)]
+def ring_pairs(count, steps, odd_up):
+    out = []
+    for j in range(count):
+        target = j + steps if (j % 2 == 1) == odd_up else j - steps
+        if not 0 <= target < count:
+            target = j ^ 1
+        out.append((j, target))
+    return out
 
 
 def swap_pairs(count, steps):
     pairs = [(j, j + steps) for j in range(1, count - steps, 2)]
-    met = {j for pair in pairs for j in pair}
-    rest = [j for j in range(count) if j not in met]
-    low = [j for j in rest if j < count // 2]
-    high = [j for j in rest if j >= count // 2]
-    groups = [low, high] if len(low) != 1 and len(high) != 1 else [rest]
-    fill = [edge for group in groups for edge in cycle_within(group)]
-    return pairs + [(b, a) for a, b in pairs] + fill
-
-
-def ring_pairs(count, steps):
-    out = []
-    for j in range(count):
-        target = j + steps if j % 2 else j - steps
-        if not 0 <= target < count:
-            target = j - 1 if j % 2 else j + 1
-        out.append((j, target))
-    return out
-
-
-def pair_mates(count):
+    return pairs + [(b, a) for a, b in pairs]
+
+
+def mate_pairs(count):
     return [(j, j ^ 1) for j in range(count)]
+
+
+def send(value, pairs):
+    blocks, groups = lax.axis_size("ctx"), lax.axis_size("head")
+    spare = 1 if groups % 2 == 0 else 0
+    rest = sorted(set(range(blocks)) - {a for a, _ in pairs})
+    wide = [(a * groups + g, b * groups + g) for a, b in pairs for g in range(groups)]
+    wide += [(a * groups + g, a * groups + (g ^ spare)) for a in rest for g in range(groups)]
+    return lax.ppermute(value, ("ctx", "head"), wide)
 
 
 def doc_edges(lengths_ref, base, rows):
@@ -82,41 +81,80 @@
     return lax.dot_general(a, b, (contract, ((), ())), preferred_element_type=F32)
 
 
-def states_kernel(
+def masked_rows(rows, scales, low, high):
+    wide = jnp.concatenate([scales] * (rows.shape[1] // HD), axis=1)
+    local = lax.broadcasted_iota(jnp.int32, rows.shape, 0)
+    return jnp.where((local >= low) & (local < high), rows.astype(F32) * wide, 0.0).astype(BF16)
+
+
+def store_heads(out_ref, product):
+    for h in range(out_ref.shape[0]):
+        out_ref[h] = product[h * HD : (h + 1) * HD, h * HD : (h + 1) * HD]
+
+
+def trade_kernel(lengths_hbm, q_hbm, k_hbm, v_hbm, g_hbm, other_ref, left_ref, right_ref, lengths_ref, sems):
+    rows = left_ref.shape[0]
+    place = lax.axis_index("ctx")
+    odd = place % 2 == 1
+    copy = pltpu.make_async_copy(lengths_hbm, lengths_ref, sems.at[0])
+    copy.start()
+
+    @pl.when(odd)
+    def _():
+        pltpu.make_async_copy(q_hbm, left_ref, sems.at[1]).start()
+        pltpu.make_async_copy(g_hbm, right_ref, sems.at[2]).start()
+
+    @pl.when(jnp.logical_not(odd))
+    def _():
+        pltpu.make_async_copy(k_hbm, left_ref, sems.at[1]).start()
+        pltpu.make_async_copy(v_hbm, right_ref, sems.at[2]).start()
+
+    base = place * rows
+    copy.wait()
+    starts, _, last_start, first_finish, _ = doc_edges(lengths_ref, base, rows)
+    scales = jnp.where(odd, row_scales(row_begins(starts, base, rows)), 1.0)
+    low = jnp.where(odd, 0, last_start - base)
+    high = jnp.where(odd, first_finish - base, rows)
+    pltpu.make_async_copy(q_hbm, left_ref, sems.at[1]).wait()
+    left = masked_rows(left_ref[...], scales, low, high)
+    pltpu.make_async_copy(g_hbm, right_ref, sems.at[2]).wait()
+    store_heads(other_ref, dot(left, right_ref[...], ((0,), (0,))))
+
+
+def keep_kernel(
     lengths_hbm, q_hbm, k_hbm, v_hbm, g_hbm,
-    own_ref, other_ref, gate_ref, begin_ref, scaled_ref, k_ref, v_ref, g_ref,
+    own_ref, gate_ref, begin_ref, scaled_ref, k_ref, v_ref, g_ref,
     q_ref, lengths_ref, sems,
 ):
-    pieces = [(lengths_hbm, lengths_ref), (k_hbm, k_ref), (v_hbm, v_ref), (q_hbm, q_ref), (g_hbm, g_ref)]
+    pieces = [(lengths_hbm, lengths_ref), (q_hbm, q_ref), (k_hbm, k_ref), (v_hbm, v_ref), (g_hbm, g_ref)]
     copies = [pltpu.make_async_copy(source, target, sems.at[at]) for at, (source, target) in enumerate(pieces)]
     for copy in copies:
         copy.start()
-    rows, width = q_ref.shape
+    rows = q_ref.shape[0]
     place = lax.axis_index("ctx")
     base = place * rows
+    odd = place % 2 == 1
     copies[0].wait()
     starts, _, last_start, first_finish, _ = doc_edges(lengths_ref, base, rows)
-    odd = place % 2 == 1
     keep = jnp.where(odd, last_start < base, first_finish > base + rows)
     gate_ref[...] = jnp.full(gate_ref.shape, jnp.where(keep, 1.0, 0.0), F32)
     begin = row_begins(starts, base, rows)
     begin_ref[...] = begin
     scales = row_scales(begin)
-    local = lax.broadcasted_iota(jnp.int32, (rows, width), 0)
     copies[1].wait()
-    tail_keys = jnp.where(local >= last_start - base, k_ref[...].astype(F32), 0.0).astype(BF16)
-    copies[2].wait()
-    tail = dot(tail_keys, v_ref[...], ((0,), (0,)))
-    copies[3].wait()
-    scaled = scale_rows(q_ref[...], scales)
-    scaled_ref[...] = scaled
-    head_rows = jnp.where(local < first_finish - base, scaled.astype(F32), 0.0).astype(BF16)
-    copies[4].wait()
-    head = dot(head_rows, g_ref[...], ((0,), (0,)))
-    for h in range(width // HD):
-        part = slice(h * HD, (h + 1) * HD)
-        own_ref[h] = jnp.where(odd, tail[part, part], head[part, part])
-        other_ref[h] = jnp.where(odd, head[part, part], tail[part, part])
+    scaled_ref[...] = scale_rows(q_ref[...], scales)
+    for copy in copies[2:]:
+        copy.wait()
+
+    @pl.when(odd)
+    def _():
+        left = masked_rows(k_ref[...], jnp.ones_like(scales), last_start - base, rows)
+        store_heads(own_ref, dot(left, v_ref[...], ((0,), (0,))))
+
+    @pl.when(jnp.logical_not(odd))
+    def _():
+        left = masked_rows(scaled_ref[...], jnp.ones_like(scales), 0, first_finish - base)
+        store_heads(own_ref, dot(left, g_ref[...], ((0,), (0,))))
 
 
 def inner_kernel(
@@ -225,29 +263,38 @@
     state = jax.ShapeDtypeStruct((heads, HD, HD), F32)
     flat = jax.ShapeDtypeStruct((rows, width), BF16)
     partial = jax.ShapeDtypeStruct((rows, width), F32)
-    own, other, gate, begin, *tensors = pl.pallas_call(
-        states_kernel,
-        out_shape=(state, state, jax.ShapeDtypeStruct((1, HD), F32), jax.ShapeDtypeStruct((rows, HD), jnp.int32)) + (flat,) * 4,
+    fetch = [pltpu.VMEM((rows, width), BF16), pltpu.SMEM((docs,), jnp.int32), pltpu.SemaphoreType.DMA((5,))]
+    other = pl.pallas_call(
+        trade_kernel,
+        out_shape=state,
         in_specs=[HBM] * 5,
-        out_specs=[VMEM] * 8,
-        scratch_shapes=[pltpu.VMEM((rows, width), BF16), pltpu.SMEM((docs,), jnp.int32), pltpu.SemaphoreType.DMA((5,))],
+        out_specs=VMEM,
+        scratch_shapes=[pltpu.VMEM((rows, width), BF16)] + fetch,
         compiler_params=params,
-        cost_estimate=pl.CostEstimate(flops=2 * 2 * rows * width * width, bytes_accessed=4 * rows * width * 2, transcendentals=0),
-        name="block_states",
+        cost_estimate=pl.CostEstimate(flops=2 * rows * width * width, bytes_accessed=2 * rows * width * 2, transcendentals=0),
+        name="traded_state",
     )(*held)
-
-    def send(value, pairs):
-        return lax.ppermute(value, "ctx", pairs)
-
-    mate = send(other, pair_mates(count))
-    far = send(own, ring_pairs(count, reach))
+    mate = send(other, mate_pairs(count))
+    own, gate, begin, *tensors = pl.pallas_call(
+        keep_kernel,
+        out_shape=(state, jax.ShapeDtypeStruct((1, HD), F32), jax.ShapeDtypeStruct((rows, HD), jnp.int32)) + (flat,) * 4,
+        in_specs=[HBM] * 5,
+        out_specs=[VMEM] * 7,
+        scratch_shapes=fetch,
+        compiler_params=params,
+        cost_estimate=pl.CostEstimate(flops=2 * rows * width * width, bytes_accessed=4 * rows * width * 4, transcendentals=0),
+        name="kept_state",
+    )(*held)
+    far = [(reach, True, send(own, ring_pairs(count, reach, True)))]
     joined = own + gate[None] * mate
-    slots = [(1, True), (reach, True)]
-    received = [mate, far]
-    for steps in range(1, reach):
-        pairs = swap_pairs(count, steps) if steps % 2 else ring_pairs(count, steps)
-        slots.append((steps, steps % 2 == 0))
-        received.append(send(joined, pairs))
+    near = [
+        (steps, False, send(joined, swap_pairs(count, steps))) if steps % 2
+        else (steps, True, send(joined, ring_pairs(count, steps, True)))
+        for steps in (3, 1, 2)
+    ]
+    slots = [(1, True, mate)] + far + near
+    received = [value for _, _, value in slots]
+    slots = [(steps, odd_forward) for steps, odd_forward, _ in slots]
     inner = pl.pallas_call(
         functools.partial(inner_kernel, tuple(slots)),
         out_shape=(jax.ShapeDtypeStruct((2 * len(slots), HD), F32),) + (partial,) * 4,

time: 22.6 us -> 21 us (0.929)
  the two profiles are of different devices: /device:TPU:0 before, /device:TPU:2 now
where the time goes in v3:
time: 21 us; the launch traced here: 20.9 us
  Pallas kernels  7.18 us (34%)
  starting transfers between devices  6.52 us (31%)
  waiting for transfers between devices  6.47 us (31%)
  between operations  0.67 us (3%)
    ppermute x5, starting transfers between devices, send(): return lax.ppermute(value, ('ctx', 'head'), wide)  6.52 us
    ppermute x5, waiting for transfers between devices, send(): return lax.ppermute(value, ('ctx', 'head'), wide)  6.47 us
    pallas_call x1, Pallas kernels, body(): pl.pallas_call(functools.partial(inner_kernel, tuple(slots)), out_shape=(...  2.5 us
    pallas_call x1, Pallas kernels, body(): pl.pallas_call(outer_kernel, out_shape=(flat,) * 4, in_specs=[VMEM] * (10...  1.58 us
    pallas_call x1, Pallas kernels, body(): pl.pallas_call(trade_kernel, out_shape=state, in_specs=[HBM] * 5, out_spe...  1.56 us
    pallas_call x1, Pallas kernels, body(): pl.pallas_call(keep_kernel, out_shape=(state, jax.ShapeDtypeStruct((1, HD...  1.54 us
  transfers between devices with their start and end apart: 5, of which 2 were waited for; matrix products, arithmetic and copies ran while one was open for 0% of the time, Pallas kernels for 19%

profile of v3, /device:TPU:2, one launch (start us, length us, event | category | flops | bytes accessed | tf_op | source)
XLA Modules:
  0.0 20.9 jit_solution(303307198047935754)
XLA Ops:
  0.6 1.6 %traded_state.1 = f32[2,128,128]{2,1,0:T(8,128)S(1)} custom-call(s32[8]{0:T(128)} %lengths_hbm.5, bf16[512,256]{1,0:T(8,128)(2,1)} %q_hbm.3, bf16[512,256]{1,0:T(8,128)(2,1)} %k_hbm.3, bf16[512,256]{1,0:T(8,128)(2,1)} %v_hbm.3, bf16[512,256]{1,0:T(8,128)(2,1)} %g_hbm.3), custom_call_target="tpu_custom_call" | custom-call | flops 67108864 | bytes 524288 | tf_op jit(solution)/shard_map/traded_state/pallas_call | solution.py:267
  2.2 0.1 collective-permute-start
  2.3 1.5 %kept_state.1 = (f32[2,128,128]{2,1,0:T(8,128)S(1)}, f32[1,128]{1,0:T(1,128)S(1)}, s32[512,128]{1,0:T(8,128)S(1)}, bf16[512,256]{1,0:T(8,128)(2,1)S(1)}, bf16[51...) custom-call(s32[8]{0:T(128)} %lengths_hbm.5, bf16[512,256]{1,0:T(8,128)(2,1)} %q_hbm.3, ...), custom_call_target="tpu_custom_call" | custom-call | flops 67108864 | bytes 2097152 | tf_op jit(solution)/shard_map/kept_state/pallas_call | solution.py:278
  3.8 2.1 %collective-permute-start.1 = (f32[2,128,128]{2,1,0:T(8,128)S(1)}, f32[2,128,128]{2,1,0:T(8,128)S(1)}, u32[]{:S(2)}, u32[]{:S(2)}) collective-permute-start(f32[2,128,128]{2,1,0:T(8,128)S(1)} %get-tuple-element.26), channel_id=1, source_target_pairs={{0,2},{1,3},{2,10},{3,11},{4,6},{5,7},{6,14},{7,15},{8,0},{9,1},{1... | collective-permute-start | bytes 393224 | tf_op jit(solution)/shard_map/ppermute | solution.py:42
  6.0 2.7 %collective-permute-done.refs_4_ = f32[2,128,128]{2,1,0:T(8,128)S(1)} collective-permute-done((f32[2,128,128]{2,1,0:T(8,128)S(1)}, f32[2,128,128]{2,1,0:T(8,128)S(1)}, u32[]{:S(2)}, u32[]{:S(2)}) %collective-permute-start) | collective-permute-done | bytes 131104 | tf_op jit(solution)/shard_map/ppermute | solution.py:42
  8.7 1.4 %collective-permute-start.4 = (f32[2,128,128]{2,1,0:T(8,128)S(1)}, f32[2,128,128]{2,1,0:T(8,128)S(1)}, u32[]{:S(2)}, u32[]{:S(2)}) collective-permute-start(f32[2,128,128]{2,1,0:T(8,128)S(1)} %multiply_add_fusion), channel_id=1, source_target_pairs={{0,2},{1,3},{2,6},{3,7},{4,0},{5,1},{6,10},{7,11},{8,4},{9,5},{10,... | collective-permute-start | bytes 393224 | tf_op jit(solution)/shard_map/ppermute | solution.py:42
  10.1 0.0 collective-permute-start.3
  10.1 2.9 %collective-permute-start.2 = (f32[2,128,128]{2,1,0:T(8,128)S(1)}, f32[2,128,128]{2,1,0:T(8,128)S(1)}, u32[]{:S(2)}, u32[]{:S(2)}) collective-permute-start(f32[2,128,128]{2,1,0:T(8,128)S(1)} %multiply_add_fusion), channel_id=1, source_target_pairs={{2,8},{3,9},{6,12},{7,13},{10,16},{11,17},{14,20},{15,21},{18,24},... | collective-permute-start | bytes 393224 | tf_op jit(solution)/shard_map/ppermute | solution.py:42
  13.0 2.5 %within_block.1 = (f32[10,128]{1,0:T(8,128)S(1)}, f32[512,256]{1,0:T(8,128)S(1)}, f32[512,256]{1,0:T(8,128)S(1)}, f32[512,256]{1,0:T(8,128)S(1)}, f32[512,256]{1,0:T(8,128)S(1)}) custom-call(s32[8]{0:T(128)} %lengths_hbm.5, s32[512,128]{1,0:T(8,128)S(1)} %get-tuple-element.16.begin_ref, bf16[512,256]{1,0:T(8,128)(2,1)S(1)} %get-tuple-element.17.scaled_ref, ...), custom_call_target="tpu_custom_call" | custom-call | flops 805306368 | bytes 3145728 | tf_op jit(solution)/shard_map/within_block/pallas_call | solution.py:298
  15.5 0.0 collective-permute-done.1.refs_5_
  15.5 3.8 %collective-permute-done.4.refs_8_ = f32[2,128,128]{2,1,0:T(8,128)S(1)} collective-permute-done((f32[2,128,128]{2,1,0:T(8,128)S(1)}, f32[2,128,128]{2,1,0:T(8,128)S(1)}, u32[]{:S(2)}, u32[]{:S(2)}) %collective-permute-start.4) | collective-permute-done | bytes 131104 | tf_op jit(solution)/shard_map/ppermute | solution.py:42
  19.3 0.0 collective-permute-done.3.refs_7_
  19.3 0.0 collective-permute-done.2.refs_6_
  19.3 1.6 %across_blocks.1 = (bf16[512,256]{1,0:T(8,128)(2,1)}, bf16[512,256]{1,0:T(8,128)(2,1)}, bf16[512,256]{1,0:T(8,128)(2,1)}, bf16[512,256]{1,0:T(8,128)(2,1)}) custom-call(s32[512,128]{1,0:T(8,128)S(1)} %get-tuple-element.16.begin_ref, bf16[512,256]{1,0:T(8,128)(2,1)S(1)} %get-tuple-element.17.scaled_ref, bf16[512,256]{1,0:T(8,128)(2,1)S(1)} %get-tuple-element.18.k_ref, ...), custom_call_target="tpu_custom_call" | custom-call | flops 134217728 | bytes 4194304 | tf_op jit(solution)/shard_map/across_blocks/pallas_call | solution.py:308
  (1 shorter events, 0.0 us)
Async XLA Ops:
  2.2 6.5 %collective-permute-start = (f32[2,128,128]{2,1,0:T(8,128)S(1)}, f32[2,128,128]{2,1,0:T(8,128)S(1)}, u32[]{:S(2)}, u32[]{:S(2)}) collective-permute-start(f32[2,128,128]{2,1,0:T(8,128)S(1)} %traded_state.1), channel_id=1, source_target_pairs={{0,2},{1,3},{2,0},{3,1},{4,6},{5,7},{6,4},{7,5},{8,10},{9,11},{10,... | collective-permute-start | bytes 393224 | tf_op jit(solution)/shard_map/ppermute | solution.py:42
  3.8 11.7 %collective-permute-start.1 = (f32[2,128,128]{2,1,0:T(8,128)S(1)}, f32[2,128,128]{2,1,0:T(8,128)S(1)}, u32[]{:S(2)}, u32[]{:S(2)}) collective-permute-start(f32[2,128,128]{2,1,0:T(8,128)S(1)} %get-tuple-element.26), channel_id=1, source_target_pairs={{0,2},{1,3},{2,10},{3,11},{4,6},{5,7},{6,14},{7,15},{8,0},{9,1},{1... | collective-permute-start | bytes 393224 | tf_op jit(solution)/shard_map/ppermute | solution.py:42
  8.7 10.6 %collective-permute-start.4 = (f32[2,128,128]{2,1,0:T(8,128)S(1)}, f32[2,128,128]{2,1,0:T(8,128)S(1)}, u32[]{:S(2)}, u32[]{:S(2)}) collective-permute-start(f32[2,128,128]{2,1,0:T(8,128)S(1)} %multiply_add_fusion), channel_id=1, source_target_pairs={{0,2},{1,3},{2,6},{3,7},{4,0},{5,1},{6,10},{7,11},{8,4},{9,5},{10,... | collective-permute-start | bytes 393224 | tf_op jit(solution)/shard_map/ppermute | solution.py:42
  10.1 9.2 %collective-permute-start.3 = (f32[2,128,128]{2,1,0:T(8,128)S(1)}, f32[2,128,128]{2,1,0:T(8,128)S(1)}, u32[]{:S(2)}, u32[]{:S(2)}) collective-permute-start(f32[2,128,128]{2,1,0:T(8,128)S(1)} %multiply_add_fusion), channel_id=1, source_target_pairs={{2,4},{3,5},{6,8},{7,9},{10,12},{11,13},{14,16},{15,17},{18,20},{1... | collective-permute-start | bytes 393224 | tf_op jit(solution)/shard_map/ppermute | solution.py:42
  10.1 9.2 %collective-permute-start.2 = (f32[2,128,128]{2,1,0:T(8,128)S(1)}, f32[2,128,128]{2,1,0:T(8,128)S(1)}, u32[]{:S(2)}, u32[]{:S(2)}) collective-permute-start(f32[2,128,128]{2,1,0:T(8,128)S(1)} %multiply_add_fusion), channel_id=1, source_target_pairs={{2,8},{3,9},{6,12},{7,13},{10,16},{11,17},{14,20},{15,21},{18,24},... | collective-permute-start | bytes 393224 | tf_op jit(solution)/shard_map/ppermute | solution.py:42

commit v4 on v2

--- a/solution.py
+++ b/solution.py
@@ -14,33 +14,37 @@
 VMEM = pl.BlockSpec(memory_space=pltpu.VMEM)
 
 
-def cycle_within(nodes):
-    return [(node, nodes[(at + 1) % len(nodes)]) for at, node in enumerate(nodes)]
+def ring_pairs(count, steps, odd_up):
+    out = []
+    for j in range(count):
+        target = j + steps if (j % 2 == 1) == odd_up else j - steps
+        if not 0 <= target < count:
+            target = j ^ 1
+        out.append((j, target))
+    return out
 
 
 def swap_pairs(count, steps):
     pairs = [(j, j + steps) for j in range(1, count - steps, 2)]
-    met = {j for pair in pairs for j in pair}
-    rest = [j for j in range(count) if j not in met]
-    low = [j for j in rest if j < count // 2]
-    high = [j for j in rest if j >= count // 2]
-    groups = [low, high] if len(low) != 1 and len(high) != 1 else [rest]
-    fill = [edge for group in groups for edge in cycle_within(group)]
-    return pairs + [(b, a) for a, b in pairs] + fill
-
-
-def ring_pairs(count, steps):
-    out = []
-    for j in range(count):
-        target = j + steps if j % 2 else j - steps
-        if not 0 <= target < count:
-            target = j - 1 if j % 2 else j + 1
-        out.append((j, target))
-    return out
-
-
-def pair_mates(count):
+    return pairs + [(b, a) for a, b in pairs]
+
+
+def group_pairs(count, steps, first):
+    pairs = [(j, j + steps) for j in range(count - steps) if j // steps % 2 == first]
+    return pairs + [(b, a) for a, b in pairs]
+
+
+def mate_pairs(count):
     return [(j, j ^ 1) for j in range(count)]
+
+
+def send(value, pairs):
+    blocks, groups = lax.axis_size("ctx"), lax.axis_size("head")
+    spare = 1 if groups % 2 == 0 else 0
+    rest = sorted(set(range(blocks)) - {a for a, _ in pairs})
+    wide = [(a * groups + g, b * groups + g) for a, b in pairs for g in range(groups)]
+    wide += [(a * groups + g, a * groups + (g ^ spare)) for a in rest for g in range(groups)]
+    return lax.ppermute(value, ("ctx", "head"), wide)
 
 
 def doc_edges(lengths_ref, base, rows):
@@ -83,9 +87,8 @@
 
 
 def states_kernel(
-    lengths_hbm, q_hbm, k_hbm, v_hbm, g_hbm,
-    own_ref, other_ref, gate_ref, begin_ref, scaled_ref, k_ref, v_ref, g_ref,
-    q_ref, lengths_ref, sems,
+    reach, lengths_hbm, q_hbm, k_hbm, v_hbm, g_hbm, own_ref, other_ref, even_ref, odd_ref, gate_ref, pick_ref,
+    q_ref, k_ref, v_ref, g_ref, lengths_ref, sems,
 ):
     pieces = [(lengths_hbm, lengths_ref), (k_hbm, k_ref), (v_hbm, v_ref), (q_hbm, q_ref), (g_hbm, g_ref)]
     copies = [pltpu.make_async_copy(source, target, sems.at[at]) for at, (source, target) in enumerate(pieces)]
@@ -97,47 +100,72 @@
     copies[0].wait()
     starts, _, last_start, first_finish, _ = doc_edges(lengths_ref, base, rows)
     odd = place % 2 == 1
+    upper = place // reach % 2 == 1
     keep = jnp.where(odd, last_start < base, first_finish > base + rows)
     gate_ref[...] = jnp.full(gate_ref.shape, jnp.where(keep, 1.0, 0.0), F32)
-    begin = row_begins(starts, base, rows)
-    begin_ref[...] = begin
-    scales = row_scales(begin)
+    at_end = (place == 0) | (place == lax.axis_size("ctx") - 1)
+    for at, picked in enumerate((odd == upper, at_end)):
+        pick_ref[at : at + 1, :] = jnp.full((1, HD), jnp.where(picked, 1.0, 0.0), F32)
+    scales = row_scales(row_begins(starts, base, rows))
     local = lax.broadcasted_iota(jnp.int32, (rows, width), 0)
     copies[1].wait()
     tail_keys = jnp.where(local >= last_start - base, k_ref[...].astype(F32), 0.0).astype(BF16)
     copies[2].wait()
     tail = dot(tail_keys, v_ref[...], ((0,), (0,)))
     copies[3].wait()
-    scaled = scale_rows(q_ref[...], scales)
-    scaled_ref[...] = scaled
-    head_rows = jnp.where(local < first_finish - base, scaled.astype(F32), 0.0).astype(BF16)
+    scaled = q_ref[...].astype(F32) * jnp.concatenate([scales] * (width // HD), axis=1)
+    head_rows = jnp.where(local < first_finish - base, scaled, 0.0).astype(BF16)
     copies[4].wait()
     head = dot(head_rows, g_ref[...], ((0,), (0,)))
     for h in range(width // HD):
         part = slice(h * HD, (h + 1) * HD)
         own_ref[h] = jnp.where(odd, tail[part, part], head[part, part])
         other_ref[h] = jnp.where(odd, head[part, part], tail[part, part])
+        even_ref[h] = jnp.where(upper, head[part, part], tail[part, part])
+        odd_ref[h] = jnp.where(upper, tail[part, part], head[part, part])
 
 
 def inner_kernel(
-    slots, lengths_hbm, begin_ref, scaled_ref, k_ref, v_ref, g_ref,
-    gates_ref, att_ref, gq_ref, gk_ref, gv_ref, lengths_ref, sem,
+    slots, reach, lengths_hbm, q_hbm, k_hbm, v_hbm, g_hbm,
+    gates_ref, begin_ref, scaled_ref, k_ref, v_ref, g_ref, att_ref, gq_ref, gk_ref, gv_ref,
+    q_ref, lengths_ref, sems,
 ):
-    copy = pltpu.make_async_copy(lengths_hbm, lengths_ref, sem)
-    copy.start()
+    pieces = [(lengths_hbm, lengths_ref), (q_hbm, q_ref), (k_hbm, k_ref), (v_hbm, v_ref), (g_hbm, g_ref)]
+    copies = [pltpu.make_async_copy(source, target, sems.at[at]) for at, (source, target) in enumerate(pieces)]
+    for copy in copies:
+        copy.start()
     rows, width = scaled_ref.shape
-    copy.wait()
     place = lax.axis_index("ctx")
     base = place * rows
-    _, first_start, _, _, last_finish = doc_edges(lengths_ref, base, rows)
     odd = place % 2 == 1
-    gates = []
-    for steps, odd_forward in slots:
-        forward = odd if odd_forward else jnp.logical_not(odd)
-        gates.append(forward & (first_start < (place - steps + 1) * rows))
-        gates.append(jnp.logical_not(forward) & (last_finish > (place + steps) * rows))
-    for at, gate in enumerate(gates):
-        gates_ref[at : at + 1, :] = jnp.full((1, HD), jnp.where(gate, 1.0, 0.0), F32)
+    upper = place // reach % 2 == 1
+    copies[0].wait()
+    starts, first_start, _, _, last_finish = doc_edges(lengths_ref, base, rows)
+    even, lower = jnp.logical_not(odd), jnp.logical_not(upper)
+    kinds = {"odd": odd, "ring": odd, "even": even, "relay": even, "upper": upper, "lower": lower}
+    by_end = (place == 1) | (place == lax.axis_size("ctx") - 2)
+
+    def gate_of(steps, kind):
+        forward = kinds[kind]
+        before = forward & (first_start < (place - steps + 1) * rows)
+        after = jnp.logical_not(forward) & (last_finish > (place + steps) * rows)
+        return before, after
+
+    for at, (steps, kind) in enumerate(slots):
+        before, after = gate_of(steps, kind)
+        if kind == "relay":
+            before, after = before & jnp.logical_not(by_end), after & jnp.logical_not(by_end)
+        if kind == "ring":
+            far_before, far_after = gate_of(reach - 1, "relay")
+            before, after = before | (by_end & far_before), after | (by_end & far_after)
+        gates_ref[2 * at : 2 * at + 1, :] = jnp.full((1, HD), jnp.where(before, 1.0, 0.0), F32)
+        gates_ref[2 * at + 1 : 2 * at + 2, :] = jnp.full((1, HD), jnp.where(after, 1.0, 0.0), F32)
+    begin_rows = row_begins(starts, base, rows)
+    begin_ref[...] = begin_rows
+    copies[1].wait()
+    scaled_ref[...] = scale_rows(q_ref[...], row_scales(begin_rows))
+    for copy in copies[2:]:
+        copy.wait()
     tile = min(256, rows)
     for at in range(0, rows, tile):
         reach = at + tile
@@ -184,7 +212,7 @@
     return dot(rows, state[0], contract) + dot(rows, state[1], contract)
 
 
-def outer_kernel(begin_ref, scaled_ref, k_ref, v_ref, g_ref, gates_ref, *refs):
+def outer_kernel(gates_ref, begin_ref, scaled_ref, k_ref, v_ref, g_ref, *refs):
     out_hbms, out_refs, sems = refs[-9:-5], refs[-5:-1], refs[-1]
     inner_refs, slot_refs = refs[:4], refs[4:-9]
     heads = scaled_ref.shape[1] // HD
@@ -225,39 +253,47 @@
     state = jax.ShapeDtypeStruct((heads, HD, HD), F32)
     flat = jax.ShapeDtypeStruct((rows, width), BF16)
     partial = jax.ShapeDtypeStruct((rows, width), F32)
-    own, other, gate, begin, *tensors = pl.pallas_call(
-        states_kernel,
-        out_shape=(state, state, jax.ShapeDtypeStruct((1, HD), F32), jax.ShapeDtypeStruct((rows, HD), jnp.int32)) + (flat,) * 4,
+    fetch = [pltpu.SMEM((docs,), jnp.int32), pltpu.SemaphoreType.DMA((5,))]
+    own, other, even, odd, gate, pick = pl.pallas_call(
+        functools.partial(states_kernel, reach),
+        out_shape=(state,) * 4 + (jax.ShapeDtypeStruct((1, HD), F32), jax.ShapeDtypeStruct((2, HD), F32)),
         in_specs=[HBM] * 5,
-        out_specs=[VMEM] * 8,
-        scratch_shapes=[pltpu.VMEM((rows, width), BF16), pltpu.SMEM((docs,), jnp.int32), pltpu.SemaphoreType.DMA((5,))],
+        out_specs=[VMEM] * 6,
+        scratch_shapes=[pltpu.VMEM((rows, width), BF16)] * 4 + fetch,
         compiler_params=params,
         cost_estimate=pl.CostEstimate(flops=2 * 2 * rows * width * width, bytes_accessed=4 * rows * width * 2, transcendentals=0),
         name="block_states",
     )(*held)
-
-    def send(value, pairs):
-        return lax.ppermute(value, "ctx", pairs)
-
-    mate = send(other, pair_mates(count))
-    far = send(own, ring_pairs(count, reach))
+    mate = send(other, mate_pairs(count))
+    far = [
+        (reach, "upper", send(even, group_pairs(count, reach, 0))),
+        (reach, "lower", send(odd, group_pairs(count, reach, 1))),
+    ]
     joined = own + gate[None] * mate
-    slots = [(1, True), (reach, True)]
-    received = [mate, far]
-    for steps in range(1, reach):
-        pairs = swap_pairs(count, steps) if steps % 2 else ring_pairs(count, steps)
-        slots.append((steps, steps % 2 == 0))
-        received.append(send(joined, pairs))
-    inner = pl.pallas_call(
-        functools.partial(inner_kernel, tuple(slots)),
-        out_shape=(jax.ShapeDtypeStruct((2 * len(slots), HD), F32),) + (partial,) * 4,
-        in_specs=[HBM] + [VMEM] * 5,
-        out_specs=[VMEM] * 5,
-        scratch_shapes=[pltpu.SMEM((docs,), jnp.int32), pltpu.SemaphoreType.DMA(())],
+    ringed = jnp.where(pick[1] > 0.5, far[0][2], joined)
+    high_far, _ = lax.optimization_barrier((far[1][2], ringed))
+    relayed = jnp.where(pick[0] > 0.5, far[0][2], high_far)
+    near = [
+        (reach - 1, "relay", send(relayed, mate_pairs(count)[2:-2])),
+        (2, "ring", send(ringed, ring_pairs(count, 2, True))),
+        *[(steps, "odd", send(joined, ring_pairs(count, steps, True))) for steps in range(4, reach - 1, 2)],
+        *[(steps, "even", send(joined, swap_pairs(count, steps))) for steps in range(1, reach - 1, 2)],
+    ]
+    slots = [(1, "odd", mate)] + far + near
+    received = [value for _, _, value in slots]
+    slots = [(steps, kind) for steps, kind, _ in slots]
+    gates, begin, *tensors = pl.pallas_call(
+        functools.partial(inner_kernel, tuple(slots), reach),
+        out_shape=(jax.ShapeDtypeStruct((2 * len(slots), HD), F32), jax.ShapeDtypeStruct((rows, HD), jnp.int32))
+        + (flat,) * 4
+        + (partial,) * 4,
+        in_specs=[HBM] * 5,
+        out_specs=[VMEM] * 10,
+        scratch_shapes=[pltpu.VMEM((rows, width), BF16)] + fetch,
         compiler_params=params,
         cost_estimate=pl.CostEstimate(flops=6 * 2 * rows * rows * width, bytes_accessed=4 * rows * width * 6, transcendentals=0),
         name="within_block",
-    )(held[0], begin, *tensors)
+    )(*held)
     return pl.pallas_call(
         outer_kernel,
         out_shape=(flat,) * 4,
@@ -267,7 +303,7 @@
         compiler_params=params,
         cost_estimate=pl.CostEstimate(flops=4 * 2 * rows * width * HD, bytes_accessed=4 * rows * width * 8, transcendentals=0),
         name="across_blocks",
-    )(begin, *tensors, *inner, *received)
+    )(gates, begin, *tensors, *received)
 
 
 def solution(mesh):

time: 22.6 us -> 19.2 us (0.85)
  starting transfers between devices: 10.4 us -> 7.69 us
  waiting for transfers between devices: 5.51 us -> 4.04 us
  Pallas kernels: 5.89 us -> 6.59 us
    ppermute x5 -> x6, starting transfers between devices: 10.4 us -> 7.69 us  [send(): return lax.ppermute(value, ('ctx', 'head'), wide)]
    ppermute x5 -> x6, waiting for transfers between devices: 5.51 us -> 4.04 us  [send(): return lax.ppermute(value, ('ctx', 'head'), wide)]
    pallas_call x2, Pallas kernels: 4.31 us -> 5.01 us  [the longest x1 3.06 us: body(): pl.pallas_call(functools.partial(inner_kernel, tuple(slots), reach), out_...]
  transfers between devices with their start and end apart: 5 -> 6, of which waited for: 2 -> 3; matrix products, arithmetic and copies ran while one was open for 0% -> 0% of each run, Pallas kernels for 11% -> 16%
where the time goes in v4:
time: 19.2 us; the launch traced here: 19.1 us
  starting transfers between devices  7.69 us (40%)
  Pallas kernels  6.59 us (34%)
  waiting for transfers between devices  4.04 us (21%)
  between operations  0.68 us (4%)
    ppermute x6, starting transfers between devices, send(): return lax.ppermute(value, ('ctx', 'head'), wide)  7.69 us
    ppermute x6, waiting for transfers between devices, send(): return lax.ppermute(value, ('ctx', 'head'), wide)  4.04 us
    pallas_call x1, Pallas kernels, body(): pl.pallas_call(functools.partial(inner_kernel, tuple(slots), reach), out_...  3.06 us
    pallas_call x1, Pallas kernels, body(): pl.pallas_call(functools.partial(states_kernel, reach), out_shape=(state,...  1.95 us
    pallas_call x1, Pallas kernels, body(): pl.pallas_call(outer_kernel, out_shape=(flat,) * 4, in_specs=[VMEM] * (10...  1.58 us
  transfers between devices with their start and end apart: 6, of which 3 were waited for; matrix products, arithmetic and copies ran while one was open for 0% of the time, Pallas kernels for 16%

profile of v4, /device:TPU:0, one launch (start us, length us, event | category | flops | bytes accessed | tf_op | source)
XLA Modules:
  0.0 19.1 jit_solution(870499836537584924)
XLA Ops:
  0.6 1.9 %block_states.1 = (f32[2,128,128]{2,1,0:T(8,128)S(1)}, f32[2,128,128]{2,1,0:T(8,128)S(1)}, f32[2,128,128]{2,1,0:T(8,128)S(1)}, f32[2,128,128]{2,1,0:T(8,128)S(1)...) custom-call(s32[8]{0:T(128)} %lengths_hbm.3, bf16[512,256]{1,0:T(8,128)(2,1)} %q_hbm.3, bf16[512,256]{1,0:T(8,128)(2,1)} %k_hbm.3, ...), custom_call_target="tpu_custom_call" | custom-call | flops 134217728 | bytes 1048576 | tf_op jit(solution)/shard_map/block_states/pallas_call | solution.py:257
  2.6 3.0 %collective-permute-start = (f32[2,128,128]{2,1,0:T(8,128)S(1)}, f32[2,128,128]{2,1,0:T(8,128)S(1)}, u32[]{:S(2)}, u32[]{:S(2)}) collective-permute-start(f32[2,128,128]{2,1,0:T(8,128)S(1)} %get-tuple-element.31), channel_id=1, source_target_pairs={{0,2},{1,3},{2,0},{3,1},{4,6},{5,7},{6,4},{7,5},{8,10},{9,11},{10,... | collective-permute-start | bytes 393224 | tf_op jit(solution)/shard_map/ppermute | solution.py:47
  5.6 1.6 %collective-permute-start.1 = (f32[2,128,128]{2,1,0:T(8,128)S(1)}, f32[2,128,128]{2,1,0:T(8,128)S(1)}, u32[]{:S(2)}, u32[]{:S(2)}) collective-permute-start(f32[2,128,128]{2,1,0:T(8,128)S(1)} %get-tuple-element.32), channel_id=1, source_target_pairs={{0,8},{1,9},{2,10},{3,11},{4,12},{5,13},{6,14},{7,15},{16,24},{17,... | collective-permute-start | bytes 393224 | tf_op jit(solution)/shard_map/ppermute | solution.py:47
  7.2 0.0 collective-permute-start.2
  7.2 1.9 %collective-permute-done.refs_4_ = f32[2,128,128]{2,1,0:T(8,128)S(1)} collective-permute-done((f32[2,128,128]{2,1,0:T(8,128)S(1)}, f32[2,128,128]{2,1,0:T(8,128)S(1)}, u32[]{:S(2)}, u32[]{:S(2)}) %collective-permute-start) | collective-permute-done | bytes 131104 | tf_op jit(solution)/shard_map/ppermute | solution.py:47
  9.1 1.5 %collective-permute-done.1.refs_5_ = f32[2,128,128]{2,1,0:T(8,128)S(1)} collective-permute-done((f32[2,128,128]{2,1,0:T(8,128)S(1)}, f32[2,128,128]{2,1,0:T(8,128)S(1)}, u32[]{:S(2)}, u32[]{:S(2)}) %collective-permute-start.1) | collective-permute-done | bytes 131104 | tf_op jit(solution)/shard_map/ppermute | solution.py:47
  10.6 0.1 collective-permute-start.5
  10.7 3.0 %collective-permute-start.4 = (f32[2,128,128]{2,1,0:T(8,128)S(1)}, f32[2,128,128]{2,1,0:T(8,128)S(1)}, u32[]{:S(2)}, u32[]{:S(2)}) collective-permute-start(f32[2,128,128]{2,1,0:T(8,128)S(1)} %get-tuple-element.38), channel_id=1, source_target_pairs={{0,2},{1,3},{2,6},{3,7},{4,0},{5,1},{6,10},{7,11},{8,4},{9,5},{10,... | collective-permute-start | bytes 393224 | tf_op jit(solution)/shard_map/ppermute | solution.py:47
  13.6 0.0 collective-permute-done.2.refs_6_
  13.7 0.1 collective-permute-start.3
  13.7 3.1 %within_block.1 = (f32[12,128]{1,0:T(8,128)S(1)}, s32[512,128]{1,0:T(8,128)S(1)}, bf16[512,256]{1,0:T(8,128)(2,1)S(1)}, bf16[512,256]{1,0:T(8,128)(2,1)S(1)}, bf...) custom-call(s32[8]{0:T(128)} %lengths_hbm.3, ...), custom_call_target="tpu_custom_call" | custom-call | flops 805306368 | bytes 3145728 | tf_op jit(solution)/shard_map/within_block/pallas_call | solution.py:285
  16.8 0.0 collective-permute-done.5.refs_9_
  16.8 0.7 %collective-permute-done.4.refs_8_ = f32[2,128,128]{2,1,0:T(8,128)S(1)} collective-permute-done((f32[2,128,128]{2,1,0:T(8,128)S(1)}, f32[2,128,128]{2,1,0:T(8,128)S(1)}, u32[]{:S(2)}, u32[]{:S(2)}) %collective-permute-start.4) | collective-permute-done | bytes 131104 | tf_op jit(solution)/shard_map/ppermute | solution.py:47
  17.5 0.0 collective-permute-done.3.refs_7_
  17.5 1.6 %across_blocks.1 = (bf16[512,256]{1,0:T(8,128)(2,1)}, bf16[512,256]{1,0:T(8,128)(2,1)}, bf16[512,256]{1,0:T(8,128)(2,1)}, bf16[512,256]{1,0:T(8,128)(2,1)}) custom-call(f32[12,128]{1,0:T(8,128)S(1)} %get-tuple-element.21.gates_ref, s32[512,128]{1,0:T(8,128)S(1)} %get-tuple-element.22.begin_ref, bf16[512,256]{1,0:T(8,128)(2,1)S(1)} %get-tuple-element.23.scaled_ref, ...), custom_call_target="tpu_custom_call" | custom-call | flops 134217728 | bytes 4194304 | tf_op jit(solution)/shard_map/across_blocks/pallas_call | solution.py:297
  (3 shorter events, 0.1 us)
Async XLA Ops:
  2.6 6.5 %collective-permute-start = (f32[2,128,128]{2,1,0:T(8,128)S(1)}, f32[2,128,128]{2,1,0:T(8,128)S(1)}, u32[]{:S(2)}, u32[]{:S(2)}) collective-permute-start(f32[2,128,128]{2,1,0:T(8,128)S(1)} %get-tuple-element.31), channel_id=1, source_target_pairs={{0,2},{1,3},{2,0},{3,1},{4,6},{5,7},{6,4},{7,5},{8,10},{9,11},{10,... | collective-permute-start | bytes 393224 | tf_op jit(solution)/shard_map/ppermute | solution.py:47
  5.6 5.0 %collective-permute-start.1 = (f32[2,128,128]{2,1,0:T(8,128)S(1)}, f32[2,128,128]{2,1,0:T(8,128)S(1)}, u32[]{:S(2)}, u32[]{:S(2)}) collective-permute-start(f32[2,128,128]{2,1,0:T(8,128)S(1)} %get-tuple-element.32), channel_id=1, source_target_pairs={{0,8},{1,9},{2,10},{3,11},{4,12},{5,13},{6,14},{7,15},{16,24},{17,... | collective-permute-start | bytes 393224 | tf_op jit(solution)/shard_map/ppermute | solution.py:47
  7.2 6.5 %collective-permute-start.2 = (f32[2,128,128]{2,1,0:T(8,128)S(1)}, f32[2,128,128]{2,1,0:T(8,128)S(1)}, u32[]{:S(2)}, u32[]{:S(2)}) collective-permute-start(f32[2,128,128]{2,1,0:T(8,128)S(1)} %get-tuple-element.33), channel_id=1, source_target_pairs={{8,16},{9,17},{10,18},{11,19},{12,20},{13,21},{14,22},{15,23},{16,... | collective-permute-start | bytes 393224 | tf_op jit(solution)/shard_map/ppermute | solution.py:47
  10.6 6.2 %collective-permute-start.5 = (f32[2,128,128]{2,1,0:T(8,128)S(1)}, f32[2,128,128]{2,1,0:T(8,128)S(1)}, u32[]{:S(2)}, u32[]{:S(2)}) collective-permute-start(f32[2,128,128]{2,1,0:T(8,128)S(1)} %get-tuple-element.39), channel_id=1, source_target_pairs={{2,4},{3,5},{6,8},{7,9},{10,12},{11,13},{14,16},{15,17},{18,20},{1... | collective-permute-start | bytes 393224 | tf_op jit(solution)/shard_map/ppermute | solution.py:47
  10.7 6.8 %collective-permute-start.4 = (f32[2,128,128]{2,1,0:T(8,128)S(1)}, f32[2,128,128]{2,1,0:T(8,128)S(1)}, u32[]{:S(2)}, u32[]{:S(2)}) collective-permute-start(f32[2,128,128]{2,1,0:T(8,128)S(1)} %get-tuple-element.38), channel_id=1, source_target_pairs={{0,2},{1,3},{2,6},{3,7},{4,0},{5,1},{6,10},{7,11},{8,4},{9,5},{10,... | collective-permute-start | bytes 393224 | tf_op jit(solution)/shard_map/ppermute | solution.py:47
  13.7 3.8 %collective-permute-start.3 = (f32[2,128,128]{2,1,0:T(8,128)S(1)}, f32[2,128,128]{2,1,0:T(8,128)S(1)}, u32[]{:S(2)}, u32[]{:S(2)}) collective-permute-start(f32[2,128,128]{2,1,0:T(8,128)S(1)} %broadcast_select_fusion.1), channel_id=1, source_target_pairs={{4,6},{5,7},{6,4},{7,5},{8,10},{9,11},{10,8},{11,9},{12,14},{13,15... | collective-permute-start | bytes 393224 | tf_op jit(solution)/shard_map/ppermute | solution.py:47

commit v5 on v4

--- a/solution.py
+++ b/solution.py
@@ -76,96 +76,116 @@
     return lax.rsqrt((local - begin).astype(F32) + 1.0) * HD ** (-0.5)
 
 
-def scale_rows(query, scales):
-    heads = query.shape[1] // HD
-    wide = jnp.concatenate([scales] * heads, axis=1)
-    return (query.astype(F32) * wide).astype(BF16)
-
-
 def dot(a, b, contract):
     return lax.dot_general(a, b, (contract, ((), ())), preferred_element_type=F32)
 
 
-def states_kernel(
-    reach, lengths_hbm, q_hbm, k_hbm, v_hbm, g_hbm, own_ref, other_ref, even_ref, odd_ref, gate_ref, pick_ref,
-    q_ref, k_ref, v_ref, g_ref, lengths_ref, sems,
+def scaled_rows(rows, weights):
+    return (rows.astype(F32) * jnp.concatenate([weights] * (rows.shape[1] // HD), axis=1)).astype(BF16)
+
+
+def store_product(out_ref, left, right):
+    for h in range(out_ref.shape[0]):
+        part = slice(h * HD, (h + 1) * HD)
+        out_ref[h] = dot(left[:, part], right[:, part], ((0,), (0,)))
+
+
+def gate_of(place, rows, ends, steps, forward):
+    _, first_start, _, _, last_finish = ends
+    before = forward & (first_start < (place - steps + 1) * rows)
+    after = jnp.logical_not(forward) & (last_finish > (place + steps) * rows)
+    return before, after
+
+
+def store_flags(out_ref, flags):
+    for at, flag in enumerate(flags):
+        out_ref[at : at + 1, :] = jnp.full((1, HD), jnp.where(flag, 1.0, 0.0), F32)
+
+
+def trade_kernel(
+    slots, reach, lengths_hbm, q_hbm, k_hbm, v_hbm, g_hbm,
+    other_ref, left_ref, right_ref, own_left_ref, own_right_ref, weight_ref, begin_ref, flags_ref, gates_ref,
+    lengths_ref, sems,
 ):
-    pieces = [(lengths_hbm, lengths_ref), (k_hbm, k_ref), (v_hbm, v_ref), (q_hbm, q_ref), (g_hbm, g_ref)]
-    copies = [pltpu.make_async_copy(source, target, sems.at[at]) for at, (source, target) in enumerate(pieces)]
-    for copy in copies:
-        copy.start()
-    rows, width = q_ref.shape
+    rows = left_ref.shape[0]
     place = lax.axis_index("ctx")
+    odd = place % 2 == 1
+    lengths_copy = pltpu.make_async_copy(lengths_hbm, lengths_ref, sems.at[0])
+    lengths_copy.start()
+    targets = (left_ref, right_ref, own_left_ref, own_right_ref)
+
+    def fetch(*sources):
+        return [pltpu.make_async_copy(a, b, sems.at[1 + at]) for at, (a, b) in enumerate(zip(sources, targets))]
+
+    @pl.when(odd)
+    def _():
+        for copy in fetch(q_hbm, g_hbm, k_hbm, v_hbm):
+            copy.start()
+
+    @pl.when(jnp.logical_not(odd))
+    def _():
+        for copy in fetch(k_hbm, v_hbm, q_hbm, g_hbm):
+            copy.start()
+
+    copies = fetch(q_hbm, g_hbm, k_hbm, v_hbm)
     base = place * rows
-    copies[0].wait()
-    starts, _, last_start, first_finish, _ = doc_edges(lengths_ref, base, rows)
-    odd = place % 2 == 1
+    lengths_copy.wait()
+    ends = doc_edges(lengths_ref, base, rows)
+    starts, first_start, last_start, first_finish, last_finish = ends
+    begin = row_begins(starts, base, rows)
+    begin_ref[...] = begin
+    scales = row_scales(begin)
+    local = lax.broadcasted_iota(jnp.int32, begin.shape, 0)
+    tail = jnp.where(local >= last_start - base, 1.0, 0.0)
+    head = jnp.where(local < first_finish - base, scales, 0.0)
+    weight_ref[...] = jnp.where(odd, tail, head)
+    weights = jnp.where(odd, head, tail)
+    even = jnp.logical_not(odd)
     upper = place // reach % 2 == 1
+    lower = jnp.logical_not(upper)
+    count = lax.axis_size("ctx")
     keep = jnp.where(odd, last_start < base, first_finish > base + rows)
-    gate_ref[...] = jnp.full(gate_ref.shape, jnp.where(keep, 1.0, 0.0), F32)
-    at_end = (place == 0) | (place == lax.axis_size("ctx") - 1)
-    for at, picked in enumerate((odd == upper, at_end)):
-        pick_ref[at : at + 1, :] = jnp.full((1, HD), jnp.where(picked, 1.0, 0.0), F32)
-    scales = row_scales(row_begins(starts, base, rows))
-    local = lax.broadcasted_iota(jnp.int32, (rows, width), 0)
-    copies[1].wait()
-    tail_keys = jnp.where(local >= last_start - base, k_ref[...].astype(F32), 0.0).astype(BF16)
-    copies[2].wait()
-    tail = dot(tail_keys, v_ref[...], ((0,), (0,)))
-    copies[3].wait()
-    scaled = q_ref[...].astype(F32) * jnp.concatenate([scales] * (width // HD), axis=1)
-    head_rows = jnp.where(local < first_finish - base, scaled, 0.0).astype(BF16)
-    copies[4].wait()
-    head = dot(head_rows, g_ref[...], ((0,), (0,)))
-    for h in range(width // HD):
-        part = slice(h * HD, (h + 1) * HD)
-        own_ref[h] = jnp.where(odd, tail[part, part], head[part, part])
-        other_ref[h] = jnp.where(odd, head[part, part], tail[part, part])
-        even_ref[h] = jnp.where(upper, head[part, part], tail[part, part])
-        odd_ref[h] = jnp.where(upper, tail[part, part], head[part, part])
-
-
-def inner_kernel(
-    slots, reach, lengths_hbm, q_hbm, k_hbm, v_hbm, g_hbm,
-    gates_ref, begin_ref, scaled_ref, k_ref, v_ref, g_ref, att_ref, gq_ref, gk_ref, gv_ref,
-    q_ref, lengths_ref, sems,
-):
-    pieces = [(lengths_hbm, lengths_ref), (q_hbm, q_ref), (k_hbm, k_ref), (v_hbm, v_ref), (g_hbm, g_ref)]
-    copies = [pltpu.make_async_copy(source, target, sems.at[at]) for at, (source, target) in enumerate(pieces)]
-    for copy in copies:
-        copy.start()
-    rows, width = scaled_ref.shape
-    place = lax.axis_index("ctx")
-    base = place * rows
-    odd = place % 2 == 1
-    upper = place // reach % 2 == 1
-    copies[0].wait()
-    starts, first_start, _, _, last_finish = doc_edges(lengths_ref, base, rows)
-    even, lower = jnp.logical_not(odd), jnp.logical_not(upper)
+    store_flags(flags_ref, [keep, odd == upper, (place == 0) | (place == count - 1)])
     kinds = {"odd": odd, "ring": odd, "even": even, "relay": even, "upper": upper, "lower": lower}
-    by_end = (place == 1) | (place == lax.axis_size("ctx") - 2)
-
-    def gate_of(steps, kind):
-        forward = kinds[kind]
-        before = forward & (first_start < (place - steps + 1) * rows)
-        after = jnp.logical_not(forward) & (last_finish > (place + steps) * rows)
-        return before, after
-
-    for at, (steps, kind) in enumerate(slots):
-        before, after = gate_of(steps, kind)
+    by_end = (place == 1) | (place == count - 2)
+    gates = []
+    for steps, kind in slots:
+        before, after = gate_of(place, rows, ends, steps, kinds[kind])
         if kind == "relay":
             before, after = before & jnp.logical_not(by_end), after & jnp.logical_not(by_end)
         if kind == "ring":
-            far_before, far_after = gate_of(reach - 1, "relay")
+            far_before, far_after = gate_of(place, rows, ends, reach - 1, even)
             before, after = before | (by_end & far_before), after | (by_end & far_after)
-        gates_ref[2 * at : 2 * at + 1, :] = jnp.full((1, HD), jnp.where(before, 1.0, 0.0), F32)
-        gates_ref[2 * at + 1 : 2 * at + 2, :] = jnp.full((1, HD), jnp.where(after, 1.0, 0.0), F32)
-    begin_rows = row_begins(starts, base, rows)
-    begin_ref[...] = begin_rows
+        gates += [before, after]
+    store_flags(gates_ref, gates)
+    copies[0].wait()
+    left = scaled_rows(left_ref[...], weights)
     copies[1].wait()
-    scaled_ref[...] = scale_rows(q_ref[...], row_scales(begin_rows))
-    for copy in copies[2:]:
-        copy.wait()
+    store_product(other_ref, left, right_ref[...])
+    copies[2].wait()
+    copies[3].wait()
+
+
+def keep_kernel(reach, left_ref, right_ref, weight_ref, other_ref, own_ref, even_ref, odd_ref):
+    place = lax.axis_index("ctx")
+    crossed = (place % 2 == 1) == (place // reach % 2 == 1)
+    store_product(own_ref, scaled_rows(left_ref[...], weight_ref[...]), right_ref[...])
+    own, other = own_ref[...], other_ref[...]
+    even_ref[...] = jnp.where(crossed, other, own)
+    odd_ref[...] = jnp.where(crossed, own, other)
+
+
+def inner_kernel(
+    left_ref, right_ref, own_left_ref, own_right_ref, begin_ref,
+    scaled_ref, k_ref, v_ref, g_ref, att_ref, gq_ref, gk_ref, gv_ref,
+):
+    rows, width = scaled_ref.shape
+    odd = lax.axis_index("ctx") % 2 == 1
+    left, right, own_left, own_right = left_ref[...], right_ref[...], own_left_ref[...], own_right_ref[...]
+    scaled_ref[...] = scaled_rows(jnp.where(odd, left, own_left), row_scales(begin_ref[...]))
+    k_ref[...] = jnp.where(odd, own_left, left)
+    v_ref[...] = jnp.where(odd, own_right, right)
+    g_ref[...] = jnp.where(odd, right, own_right)
     tile = min(256, rows)
     for at in range(0, rows, tile):
         reach = at + tile
@@ -253,26 +273,37 @@
     state = jax.ShapeDtypeStruct((heads, HD, HD), F32)
     flat = jax.ShapeDtypeStruct((rows, width), BF16)
     partial = jax.ShapeDtypeStruct((rows, width), F32)
-    fetch = [pltpu.SMEM((docs,), jnp.int32), pltpu.SemaphoreType.DMA((5,))]
-    own, other, even, odd, gate, pick = pl.pallas_call(
-        functools.partial(states_kernel, reach),
-        out_shape=(state,) * 4 + (jax.ShapeDtypeStruct((1, HD), F32), jax.ShapeDtypeStruct((2, HD), F32)),
+    kinds = [(1, "odd"), (reach, "upper"), (reach, "lower")] + [(reach - 1, "relay")] + [(2, "ring")] + [(steps, "odd") for steps in range(4, reach - 1, 2)] + [(steps, "even") for steps in range(1, reach - 1, 2)]
+    rows_of = lambda n, kind: jax.ShapeDtypeStruct((n, HD), kind)
+    other, left, right, own_left, own_right, weight, begin, flags, gates = pl.pallas_call(
+        functools.partial(trade_kernel, tuple(kinds), reach),
+        out_shape=(state,) + (flat,) * 4 + (rows_of(rows, F32), rows_of(rows, jnp.int32), rows_of(3, F32), rows_of(2 * len(kinds), F32)),
         in_specs=[HBM] * 5,
-        out_specs=[VMEM] * 6,
-        scratch_shapes=[pltpu.VMEM((rows, width), BF16)] * 4 + fetch,
+        out_specs=[VMEM] * 9,
+        scratch_shapes=[pltpu.SMEM((docs,), jnp.int32), pltpu.SemaphoreType.DMA((5,))],
         compiler_params=params,
-        cost_estimate=pl.CostEstimate(flops=2 * 2 * rows * width * width, bytes_accessed=4 * rows * width * 2, transcendentals=0),
-        name="block_states",
+        cost_estimate=pl.CostEstimate(flops=2 * rows * width * width, bytes_accessed=4 * rows * width * 2, transcendentals=0),
+        name="traded_state",
     )(*held)
     mate = send(other, mate_pairs(count))
+    own, even, odd = pl.pallas_call(
+        functools.partial(keep_kernel, reach),
+        out_shape=(state,) * 3,
+        in_specs=[VMEM] * 4,
+        out_specs=[VMEM] * 3,
+        compiler_params=params,
+        cost_estimate=pl.CostEstimate(flops=2 * rows * width * width, bytes_accessed=2 * rows * width * 2, transcendentals=0),
+        name="kept_state",
+    )(own_left, own_right, weight, other)
     far = [
         (reach, "upper", send(even, group_pairs(count, reach, 0))),
         (reach, "lower", send(odd, group_pairs(count, reach, 1))),
     ]
-    joined = own + gate[None] * mate
-    ringed = jnp.where(pick[1] > 0.5, far[0][2], joined)
+    joined = own + flags[0] * mate
+    joined = lax.optimization_barrier(joined)
+    ringed = jnp.where(flags[2] > 0.5, far[0][2], joined)
     high_far, _ = lax.optimization_barrier((far[1][2], ringed))
-    relayed = jnp.where(pick[0] > 0.5, far[0][2], high_far)
+    relayed = jnp.where(flags[1] > 0.5, far[0][2], high_far)
     near = [
         (reach - 1, "relay", send(relayed, mate_pairs(count)[2:-2])),
         (2, "ring", send(ringed, ring_pairs(count, 2, True))),
@@ -281,19 +312,16 @@
     ]
     slots = [(1, "odd", mate)] + far + near
     received = [value for _, _, value in slots]
-    slots = [(steps, kind) for steps, kind, _ in slots]
-    gates, begin, *tensors = pl.pallas_call(
-        functools.partial(inner_kernel, tuple(slots), reach),
-        out_shape=(jax.ShapeDtypeStruct((2 * len(slots), HD), F32), jax.ShapeDtypeStruct((rows, HD), jnp.int32))
-        + (flat,) * 4
-        + (partial,) * 4,
-        in_specs=[HBM] * 5,
-        out_specs=[VMEM] * 10,
-        scratch_shapes=[pltpu.VMEM((rows, width), BF16)] + fetch,
+    assert kinds == [(steps, kind) for steps, kind, _ in slots]
+    tensors = pl.pallas_call(
+        inner_kernel,
+        out_shape=(flat,) * 4 + (partial,) * 4,
+        in_specs=[VMEM] * 5,
+        out_specs=[VMEM] * 8,
         compiler_params=params,
         cost_estimate=pl.CostEstimate(flops=6 * 2 * rows * rows * width, bytes_accessed=4 * rows * width * 6, transcendentals=0),
         name="within_block",
-    )(*held)
+    )(left, right, own_left, own_right, begin)
     return pl.pallas_call(
         outer_kernel,
         out_shape=(flat,) * 4,

time: 19.2 us -> 18.3 us (0.953); the launches traced: 19.1 us -> 17.9 us
  waiting for transfers between devices: 4.04 us -> 5.72 us
  Pallas kernels: 6.59 us -> 5.08 us
  starting transfers between devices: 7.69 us -> 6.33 us
    ppermute x6, waiting for transfers between devices: 4.04 us -> 5.72 us  [send(): return lax.ppermute(value, ('ctx', 'head'), wide)]
    pallas_call x2 -> x3, Pallas kernels: 5.01 us -> 3.5 us  [the longest x1 1.85 us: body(): pl.pallas_call(inner_kernel, out_shape=(flat,) * 4 + (partial,) * 4, in_s...]
    ppermute x6, starting transfers between devices: 7.69 us -> 6.33 us  [send(): return lax.ppermute(value, ('ctx', 'head'), wide)]
  transfers between devices with their start and end apart: 6 -> 6, of which waited for: 3 -> 3; matrix products, arithmetic and copies ran while one was open for 0% -> 0% of each run, Pallas kernels for 16% -> 12%
where the time goes in v5:
time: 18.3 us; the launch traced here: 17.9 us
  starting transfers between devices  6.33 us (35%)
  waiting for transfers between devices  5.72 us (31%)
  Pallas kernels  5.08 us (28%)
  between operations  0.71 us (4%)
    ppermute x6, starting transfers between devices, send(): return lax.ppermute(value, ('ctx', 'head'), wide)  6.33 us
    ppermute x6, waiting for transfers between devices, send(): return lax.ppermute(value, ('ctx', 'head'), wide)  5.72 us
    pallas_call x1, Pallas kernels, body(): pl.pallas_call(inner_kernel, out_shape=(flat,) * 4 + (partial,) * 4, in_s...  1.85 us
    pallas_call x1, Pallas kernels, body(): pl.pallas_call(outer_kernel, out_shape=(flat,) * 4, in_specs=[VMEM] * (10...  1.58 us
    pallas_call x1, Pallas kernels, body(): pl.pallas_call(functools.partial(trade_kernel, tuple(kinds), reach), out_...  1.37 us
  transfers between devices with their start and end apart: 6, of which 3 were waited for; matrix products, arithmetic and copies ran while one was open for 0% of the time, Pallas kernels for 12%

profile of v5, /device:TPU:0, one launch (start us, length us, event | category | flops | bytes accessed | tf_op | source)
XLA Modules:
  0.0 17.9 jit_solution(2709470922894093533)
XLA Ops:
  0.6 1.4 %traded_state.1 = (f32[2,128,128]{2,1,0:T(8,128)S(1)}, bf16[512,256]{1,0:T(8,128)(2,1)S(1)}, bf16[512,256]{1,0:T(8,128)(2,1)S(1)}, bf16[512,256]{1,0:T(8,128)(2,...) custom-call(s32[8]{0:T(128)} %lengths_hbm.1, ...), custom_call_target="tpu_custom_call" | custom-call | flops 67108864 | bytes 1048576 | tf_op jit(solution)/shard_map/traded_state/pallas_call | solution.py:278
  2.0 3.0 %collective-permute-start = (f32[2,128,128]{2,1,0:T(8,128)S(1)}, f32[2,128,128]{2,1,0:T(8,128)S(1)}, u32[]{:S(2)}, u32[]{:S(2)}) collective-permute-start(f32[2,128,128]{2,1,0:T(8,128)S(1)} %get-tuple-element.39.other_ref), channel_id=1, source_target_pairs={{0,2},{1,3},{2,0},{3,1},{4,6},{5,7},{6,4},{7,5},{8,10},{9,11},{10,... | collective-permute-start | bytes 393224 | tf_op jit(solution)/shard_map/ppermute | solution.py:47
  5.0 0.3 %kept_state.1 = (f32[2,128,128]{2,1,0:T(8,128)S(1)}, f32[2,128,128]{2,1,0:T(8,128)S(1)}, f32[2,128,128]{2,1,0:T(8,128)S(1)}) custom-call(bf16[512,256]{1,0:T(8,128)(2,1)S(1)} %get-tuple-element.29.own_left_ref.left_ref, bf16[512,256]{1,0:T(8,128)(2,1)S(1)} %get-tuple-element.30.own_right_ref.right_ref, f32[512,128]{1,0:T(8,128)S(1)} %get-tuple-element.40.weight_ref, ...), custom_call_target="tpu_custom_call" | custom-call | flops 67108864 | bytes 524288 | tf_op jit(solution)/shard_map/kept_state/pallas_call | solution.py:289
  5.3 1.6 %collective-permute-start.1 = (f32[2,128,128]{2,1,0:T(8,128)S(1)}, f32[2,128,128]{2,1,0:T(8,128)S(1)}, u32[]{:S(2)}, u32[]{:S(2)}) collective-permute-start(f32[2,128,128]{2,1,0:T(8,128)S(1)} %get-tuple-element.41), channel_id=1, source_target_pairs={{0,8},{1,9},{2,10},{3,11},{4,12},{5,13},{6,14},{7,15},{16,24},{17,... | collective-permute-start | bytes 393224 | tf_op jit(solution)/shard_map/ppermute | solution.py:47
  6.9 0.0 collective-permute-start.2
  7.0 1.5 %collective-permute-done.refs_4_ = f32[2,128,128]{2,1,0:T(8,128)S(1)} collective-permute-done((f32[2,128,128]{2,1,0:T(8,128)S(1)}, f32[2,128,128]{2,1,0:T(8,128)S(1)}, u32[]{:S(2)}, u32[]{:S(2)}) %collective-permute-start) | collective-permute-done | bytes 131104 | tf_op jit(solution)/shard_map/ppermute | solution.py:47
  8.5 0.1 collective-permute-start.5
  8.6 1.7 %collective-permute-done.1.refs_5_ = f32[2,128,128]{2,1,0:T(8,128)S(1)} collective-permute-done((f32[2,128,128]{2,1,0:T(8,128)S(1)}, f32[2,128,128]{2,1,0:T(8,128)S(1)}, u32[]{:S(2)}, u32[]{:S(2)}) %collective-permute-start.1) | collective-permute-done | bytes 131104 | tf_op jit(solution)/shard_map/ppermute | solution.py:47
  10.4 1.5 %collective-permute-start.4 = (f32[2,128,128]{2,1,0:T(8,128)S(1)}, f32[2,128,128]{2,1,0:T(8,128)S(1)}, u32[]{:S(2)}, u32[]{:S(2)}) collective-permute-start(f32[2,128,128]{2,1,0:T(8,128)S(1)} %broadcast_select_fusion), channel_id=1, source_target_pairs={{0,2},{1,3},{2,6},{3,7},{4,0},{5,1},{6,10},{7,11},{8,4},{9,5},{10,... | collective-permute-start | bytes 393224 | tf_op jit(solution)/shard_map/ppermute | solution.py:47
  11.9 0.0 collective-permute-done.2.refs_6_
  11.9 0.1 collective-permute-start.3
  12.0 1.8 %within_block.1 = (bf16[512,256]{1,0:T(8,128)(2,1)S(1)}, bf16[512,256]{1,0:T(8,128)(2,1)S(1)}, bf16[512,256]{1,0:T(8,128)(2,1)S(1)}, bf16[512,256]{1,0:T(8,128)(...) custom-call(bf16[512,256]{1,0:T(8,128)(2,1)S(1)} %get-tuple-element., ...), custom_call_target="tpu_custom_call" | custom-call | flops 805306368 | bytes 3145728 | tf_op jit(solution)/shard_map/within_block/pallas_call | solution.py:316
  13.9 0.0 collective-permute-done.5.refs_9_
  13.9 2.4 %collective-permute-done.4.refs_8_ = f32[2,128,128]{2,1,0:T(8,128)S(1)} collective-permute-done((f32[2,128,128]{2,1,0:T(8,128)S(1)}, f32[2,128,128]{2,1,0:T(8,128)S(1)}, u32[]{:S(2)}, u32[]{:S(2)}) %collective-permute-start.4) | collective-permute-done | bytes 131104 | tf_op jit(solution)/shard_map/ppermute | solution.py:47
  16.3 0.0 collective-permute-done.3.refs_7_
  16.3 1.6 %across_blocks.1 = (bf16[512,256]{1,0:T(8,128)(2,1)}, bf16[512,256]{1,0:T(8,128)(2,1)}, bf16[512,256]{1,0:T(8,128)(2,1)}, bf16[512,256]{1,0:T(8,128)(2,1)}) custom-call(f32[12,128]{1,0:T(8,128)S(1)} %get-tuple-element.25.gates_ref, s32[512,128]{1,0:T(8,128)S(1)} %get-tuple-element.26.begin_ref, bf16[512,256]{1,0:T(8,128)(2,1)S(1)} %get-tuple-element.31.scaled_ref, ...), custom_call_target="tpu_custom_call" | custom-call | flops 134217728 | bytes 4194304 | tf_op jit(solution)/shard_map/across_blocks/pallas_call | solution.py:325
  (5 shorter events, 0.1 us)
Async XLA Ops:
  2.0 6.5 %collective-permute-start = (f32[2,128,128]{2,1,0:T(8,128)S(1)}, f32[2,128,128]{2,1,0:T(8,128)S(1)}, u32[]{:S(2)}, u32[]{:S(2)}) collective-permute-start(f32[2,128,128]{2,1,0:T(8,128)S(1)} %get-tuple-element.39.other_ref), channel_id=1, source_target_pairs={{0,2},{1,3},{2,0},{3,1},{4,6},{5,7},{6,4},{7,5},{8,10},{9,11},{10,... | collective-permute-start | bytes 393224 | tf_op jit(solution)/shard_map/ppermute | solution.py:47
  5.3 5.0 %collective-permute-start.1 = (f32[2,128,128]{2,1,0:T(8,128)S(1)}, f32[2,128,128]{2,1,0:T(8,128)S(1)}, u32[]{:S(2)}, u32[]{:S(2)}) collective-permute-start(f32[2,128,128]{2,1,0:T(8,128)S(1)} %get-tuple-element.41), channel_id=1, source_target_pairs={{0,8},{1,9},{2,10},{3,11},{4,12},{5,13},{6,14},{7,15},{16,24},{17,... | collective-permute-start | bytes 393224 | tf_op jit(solution)/shard_map/ppermute | solution.py:47
  6.9 5.0 %collective-permute-start.2 = (f32[2,128,128]{2,1,0:T(8,128)S(1)}, f32[2,128,128]{2,1,0:T(8,128)S(1)}, u32[]{:S(2)}, u32[]{:S(2)}) collective-permute-start(f32[2,128,128]{2,1,0:T(8,128)S(1)} %get-tuple-element.42), channel_id=1, source_target_pairs={{8,16},{9,17},{10,18},{11,19},{12,20},{13,21},{14,22},{15,23},{16,... | collective-permute-start | bytes 393224 | tf_op jit(solution)/shard_map/ppermute | solution.py:47
  8.5 5.3 %collective-permute-start.5 = (f32[2,128,128]{2,1,0:T(8,128)S(1)}, f32[2,128,128]{2,1,0:T(8,128)S(1)}, u32[]{:S(2)}, u32[]{:S(2)}) collective-permute-start(f32[2,128,128]{2,1,0:T(8,128)S(1)} %multiply_add_fusion), channel_id=1, source_target_pairs={{2,4},{3,5},{6,8},{7,9},{10,12},{11,13},{14,16},{15,17},{18,20},{1... | collective-permute-start | bytes 393224 | tf_op jit(solution)/shard_map/ppermute | solution.py:47
  10.4 6.0 %collective-permute-start.4 = (f32[2,128,128]{2,1,0:T(8,128)S(1)}, f32[2,128,128]{2,1,0:T(8,128)S(1)}, u32[]{:S(2)}, u32[]{:S(2)}) collective-permute-start(f32[2,128,128]{2,1,0:T(8,128)S(1)} %broadcast_select_fusion), channel_id=1, source_target_pairs={{0,2},{1,3},{2,6},{3,7},{4,0},{5,1},{6,10},{7,11},{8,4},{9,5},{10,... | collective-permute-start | bytes 393224 | tf_op jit(solution)/shard_map/ppermute | solution.py:47
  11.9 4.4 %collective-permute-start.3 = (f32[2,128,128]{2,1,0:T(8,128)S(1)}, f32[2,128,128]{2,1,0:T(8,128)S(1)}, u32[]{:S(2)}, u32[]{:S(2)}) collective-permute-start(f32[2,128,128]{2,1,0:T(8,128)S(1)} %broadcast_select_fusion.1), channel_id=1, source_target_pairs={{4,6},{5,7},{6,4},{7,5},{8,10},{9,11},{10,8},{11,9},{12,14},{13,15... | collective-permute-start | bytes 393224 | tf_op jit(solution)/shard_map/ppermute | solution.py:47

commit v6 on v5

--- a/solution.py
+++ b/solution.py
@@ -228,21 +228,34 @@
     return diagonal(blocks), diagonal(low)
 
 
-def split_dot(rows, state, contract):
-    return dot(rows, state[0], contract) + dot(rows, state[1], contract)
+def rounded(blocks):
+    return (diagonal(blocks),)
+
+
+def split_dot(rows, states, contract):
+    total = dot(rows, states[0], contract)
+    for state in states[1:]:
+        total = total + dot(rows, state, contract)
+    return total
+
+
+def gated_states(gates_ref, slot_refs, first):
+    heads = slot_refs[0].shape[0]
+    entering = [jnp.zeros((HD, HD), F32)] * heads
+    returning = [jnp.zeros((HD, HD), F32)] * heads
+    for at, slot_ref in enumerate(slot_refs, first):
+        before, after = gates_ref[2 * at : 2 * at + 1, :], gates_ref[2 * at + 1 : 2 * at + 2, :]
+        entering = [state + before * slot_ref[h] for h, state in enumerate(entering)]
+        returning = [state + after * slot_ref[h] for h, state in enumerate(returning)]
+    return entering, returning
 
 
 def outer_kernel(gates_ref, begin_ref, scaled_ref, k_ref, v_ref, g_ref, *refs):
     out_hbms, out_refs, sems = refs[-9:-5], refs[-5:-1], refs[-1]
     inner_refs, slot_refs = refs[:4], refs[4:-9]
     heads = scaled_ref.shape[1] // HD
-    entering = [jnp.zeros((HD, HD), F32)] * heads
-    returning = [jnp.zeros((HD, HD), F32)] * heads
-    for at, slot_ref in enumerate(slot_refs):
-        before, after = gates_ref[2 * at : 2 * at + 1, :], gates_ref[2 * at + 1 : 2 * at + 2, :]
-        entering = [state + before * slot_ref[h] for h, state in enumerate(entering)]
-        returning = [state + after * slot_ref[h] for h, state in enumerate(returning)]
-    entering, returning = split(entering), split(returning)
+    entering, returning = gated_states(gates_ref, slot_refs, 0)
+    entering, returning = rounded(entering), rounded(returning)
     copies = [pltpu.make_async_copy(out_refs[at], out_hbms[at], sems.at[at]) for at in range(4)]
     attended = inner_refs[0][...] + split_dot(scaled_ref[...], entering, ((1,), (0,)))
     out_refs[0][...] = attended.astype(BF16)

time: 18.3 us -> 18 us (0.984)
  Pallas kernels: 5.08 us -> 4.83 us
    pallas_call x1, Pallas kernels: 1.58 us -> 1.34 us  [body(): pl.pallas_call(outer_kernel, out_shape=(flat,) * 4, in_specs=[VMEM] * (10...]
where the time goes in v6:
time: 18 us; the launch traced here: 17.7 us
  starting transfers between devices  6.33 us (35%)
  waiting for transfers between devices  5.72 us (32%)
  Pallas kernels  4.83 us (27%)
  between operations  0.71 us (4%)
    ppermute x6, starting transfers between devices, send(): return lax.ppermute(value, ('ctx', 'head'), wide)  6.33 us
    ppermute x6, waiting for transfers between devices, send(): return lax.ppermute(value, ('ctx', 'head'), wide)  5.72 us
    pallas_call x1, Pallas kernels, body(): pl.pallas_call(inner_kernel, out_shape=(flat,) * 4 + (partial,) * 4, in_s...  1.85 us
    pallas_call x1, Pallas kernels, body(): pl.pallas_call(functools.partial(trade_kernel, tuple(kinds), reach), out_...  1.37 us
    pallas_call x1, Pallas kernels, body(): pl.pallas_call(outer_kernel, out_shape=(flat,) * 4, in_specs=[VMEM] * (10...  1.34 us
  transfers between devices with their start and end apart: 6, of which 3 were waited for; matrix products, arithmetic and copies ran while one was open for 0% of the time, Pallas kernels for 12%

profile of v6, /device:TPU:0, one launch (start us, length us, event | category | flops | bytes accessed | tf_op | source)
XLA Modules:
  0.0 17.7 jit_solution(5390926806442693088)
XLA Ops:
  0.6 1.4 %traded_state.1 = (f32[2,128,128]{2,1,0:T(8,128)S(1)}, bf16[512,256]{1,0:T(8,128)(2,1)S(1)}, bf16[512,256]{1,0:T(8,128)(2,1)S(1)}, bf16[512,256]{1,0:T(8,128)(2,...) custom-call(s32[8]{0:T(128)} %lengths_hbm.1, ...), custom_call_target="tpu_custom_call" | custom-call | flops 67108864 | bytes 1048576 | tf_op jit(solution)/shard_map/traded_state/pallas_call | solution.py:291
  2.0 3.0 %collective-permute-start = (f32[2,128,128]{2,1,0:T(8,128)S(1)}, f32[2,128,128]{2,1,0:T(8,128)S(1)}, u32[]{:S(2)}, u32[]{:S(2)}) collective-permute-start(f32[2,128,128]{2,1,0:T(8,128)S(1)} %get-tuple-element.39.other_ref), channel_id=1, source_target_pairs={{0,2},{1,3},{2,0},{3,1},{4,6},{5,7},{6,4},{7,5},{8,10},{9,11},{10,... | collective-permute-start | bytes 393224 | tf_op jit(solution)/shard_map/ppermute | solution.py:47
  5.0 0.3 %kept_state.1 = (f32[2,128,128]{2,1,0:T(8,128)S(1)}, f32[2,128,128]{2,1,0:T(8,128)S(1)}, f32[2,128,128]{2,1,0:T(8,128)S(1)}) custom-call(bf16[512,256]{1,0:T(8,128)(2,1)S(1)} %get-tuple-element.29.own_left_ref.left_ref, bf16[512,256]{1,0:T(8,128)(2,1)S(1)} %get-tuple-element.30.own_right_ref.right_ref, f32[512,128]{1,0:T(8,128)S(1)} %get-tuple-element.40.weight_ref, ...), custom_call_target="tpu_custom_call" | custom-call | flops 67108864 | bytes 524288 | tf_op jit(solution)/shard_map/kept_state/pallas_call | solution.py:302
  5.3 1.6 %collective-permute-start.1 = (f32[2,128,128]{2,1,0:T(8,128)S(1)}, f32[2,128,128]{2,1,0:T(8,128)S(1)}, u32[]{:S(2)}, u32[]{:S(2)}) collective-permute-start(f32[2,128,128]{2,1,0:T(8,128)S(1)} %get-tuple-element.41), channel_id=1, source_target_pairs={{0,8},{1,9},{2,10},{3,11},{4,12},{5,13},{6,14},{7,15},{16,24},{17,... | collective-permute-start | bytes 393224 | tf_op jit(solution)/shard_map/ppermute | solution.py:47
  6.9 0.0 collective-permute-start.2
  7.0 1.5 %collective-permute-done.refs_4_ = f32[2,128,128]{2,1,0:T(8,128)S(1)} collective-permute-done((f32[2,128,128]{2,1,0:T(8,128)S(1)}, f32[2,128,128]{2,1,0:T(8,128)S(1)}, u32[]{:S(2)}, u32[]{:S(2)}) %collective-permute-start) | collective-permute-done | bytes 131104 | tf_op jit(solution)/shard_map/ppermute | solution.py:47
  8.5 0.1 collective-permute-start.5
  8.6 1.7 %collective-permute-done.1.refs_5_ = f32[2,128,128]{2,1,0:T(8,128)S(1)} collective-permute-done((f32[2,128,128]{2,1,0:T(8,128)S(1)}, f32[2,128,128]{2,1,0:T(8,128)S(1)}, u32[]{:S(2)}, u32[]{:S(2)}) %collective-permute-start.1) | collective-permute-done | bytes 131104 | tf_op jit(solution)/shard_map/ppermute | solution.py:47
  10.4 1.5 %collective-permute-start.4 = (f32[2,128,128]{2,1,0:T(8,128)S(1)}, f32[2,128,128]{2,1,0:T(8,128)S(1)}, u32[]{:S(2)}, u32[]{:S(2)}) collective-permute-start(f32[2,128,128]{2,1,0:T(8,128)S(1)} %broadcast_select_fusion), channel_id=1, source_target_pairs={{0,2},{1,3},{2,6},{3,7},{4,0},{5,1},{6,10},{7,11},{8,4},{9,5},{10,... | collective-permute-start | bytes 393224 | tf_op jit(solution)/shard_map/ppermute | solution.py:47
  11.9 0.0 collective-permute-done.2.refs_6_
  11.9 0.1 collective-permute-start.3
  12.0 1.8 %within_block.1 = (bf16[512,256]{1,0:T(8,128)(2,1)S(1)}, bf16[512,256]{1,0:T(8,128)(2,1)S(1)}, bf16[512,256]{1,0:T(8,128)(2,1)S(1)}, bf16[512,256]{1,0:T(8,128)(...) custom-call(bf16[512,256]{1,0:T(8,128)(2,1)S(1)} %get-tuple-element., ...), custom_call_target="tpu_custom_call" | custom-call | flops 805306368 | bytes 3145728 | tf_op jit(solution)/shard_map/within_block/pallas_call | solution.py:329
  13.9 0.0 collective-permute-done.5.refs_9_
  13.9 2.4 %collective-permute-done.4.refs_8_ = f32[2,128,128]{2,1,0:T(8,128)S(1)} collective-permute-done((f32[2,128,128]{2,1,0:T(8,128)S(1)}, f32[2,128,128]{2,1,0:T(8,128)S(1)}, u32[]{:S(2)}, u32[]{:S(2)}) %collective-permute-start.4) | collective-permute-done | bytes 131104 | tf_op jit(solution)/shard_map/ppermute | solution.py:47
  16.3 0.0 collective-permute-done.3.refs_7_
  16.3 1.3 %across_blocks.1 = (bf16[512,256]{1,0:T(8,128)(2,1)}, bf16[512,256]{1,0:T(8,128)(2,1)}, bf16[512,256]{1,0:T(8,128)(2,1)}, bf16[512,256]{1,0:T(8,128)(2,1)}) custom-call(f32[12,128]{1,0:T(8,128)S(1)} %get-tuple-element.25.gates_ref, s32[512,128]{1,0:T(8,128)S(1)} %get-tuple-element.26.begin_ref, bf16[512,256]{1,0:T(8,128)(2,1)S(1)} %get-tuple-element.31.scaled_ref, ...), custom_call_target="tpu_custom_call" | custom-call | flops 134217728 | bytes 4194304 | tf_op jit(solution)/shard_map/across_blocks/pallas_call | solution.py:338
  (5 shorter events, 0.1 us)
Async XLA Ops:
  2.0 6.5 %collective-permute-start = (f32[2,128,128]{2,1,0:T(8,128)S(1)}, f32[2,128,128]{2,1,0:T(8,128)S(1)}, u32[]{:S(2)}, u32[]{:S(2)}) collective-permute-start(f32[2,128,128]{2,1,0:T(8,128)S(1)} %get-tuple-element.39.other_ref), channel_id=1, source_target_pairs={{0,2},{1,3},{2,0},{3,1},{4,6},{5,7},{6,4},{7,5},{8,10},{9,11},{10,... | collective-permute-start | bytes 393224 | tf_op jit(solution)/shard_map/ppermute | solution.py:47
  5.3 5.0 %collective-permute-start.1 = (f32[2,128,128]{2,1,0:T(8,128)S(1)}, f32[2,128,128]{2,1,0:T(8,128)S(1)}, u32[]{:S(2)}, u32[]{:S(2)}) collective-permute-start(f32[2,128,128]{2,1,0:T(8,128)S(1)} %get-tuple-element.41), channel_id=1, source_target_pairs={{0,8},{1,9},{2,10},{3,11},{4,12},{5,13},{6,14},{7,15},{16,24},{17,... | collective-permute-start | bytes 393224 | tf_op jit(solution)/shard_map/ppermute | solution.py:47
  6.9 5.0 %collective-permute-start.2 = (f32[2,128,128]{2,1,0:T(8,128)S(1)}, f32[2,128,128]{2,1,0:T(8,128)S(1)}, u32[]{:S(2)}, u32[]{:S(2)}) collective-permute-start(f32[2,128,128]{2,1,0:T(8,128)S(1)} %get-tuple-element.42), channel_id=1, source_target_pairs={{8,16},{9,17},{10,18},{11,19},{12,20},{13,21},{14,22},{15,23},{16,... | collective-permute-start | bytes 393224 | tf_op jit(solution)/shard_map/ppermute | solution.py:47
  8.5 5.3 %collective-permute-start.5 = (f32[2,128,128]{2,1,0:T(8,128)S(1)}, f32[2,128,128]{2,1,0:T(8,128)S(1)}, u32[]{:S(2)}, u32[]{:S(2)}) collective-permute-start(f32[2,128,128]{2,1,0:T(8,128)S(1)} %multiply_add_fusion), channel_id=1, source_target_pairs={{2,4},{3,5},{6,8},{7,9},{10,12},{11,13},{14,16},{15,17},{18,20},{1... | collective-permute-start | bytes 393224 | tf_op jit(solution)/shard_map/ppermute | solution.py:47
  10.4 6.0 %collective-permute-start.4 = (f32[2,128,128]{2,1,0:T(8,128)S(1)}, f32[2,128,128]{2,1,0:T(8,128)S(1)}, u32[]{:S(2)}, u32[]{:S(2)}) collective-permute-start(f32[2,128,128]{2,1,0:T(8,128)S(1)} %broadcast_select_fusion), channel_id=1, source_target_pairs={{0,2},{1,3},{2,6},{3,7},{4,0},{5,1},{6,10},{7,11},{8,4},{9,5},{10,... | collective-permute-start | bytes 393224 | tf_op jit(solution)/shard_map/ppermute | solution.py:47
  11.9 4.4 %collective-permute-start.3 = (f32[2,128,128]{2,1,0:T(8,128)S(1)}, f32[2,128,128]{2,1,0:T(8,128)S(1)}, u32[]{:S(2)}, u32[]{:S(2)}) collective-permute-start(f32[2,128,128]{2,1,0:T(8,128)S(1)} %broadcast_select_fusion.1), channel_id=1, source_target_pairs={{4,6},{5,7},{6,4},{7,5},{8,10},{9,11},{10,8},{11,9},{12,14},{13,15... | collective-permute-start | bytes 393224 | tf_op jit(solution)/shard_map/ppermute | solution.py:47

commit v7 on v5

--- a/solution.py
+++ b/solution.py
@@ -14,10 +14,10 @@
 VMEM = pl.BlockSpec(memory_space=pltpu.VMEM)
 
 
-def ring_pairs(count, steps, odd_up):
+def ring_pairs(count, steps):
     out = []
     for j in range(count):
-        target = j + steps if (j % 2 == 1) == odd_up else j - steps
+        target = j + steps if j % 2 else j - steps
         if not 0 <= target < count:
             target = j ^ 1
         out.append((j, target))
@@ -214,22 +214,17 @@
             gv_ref[at:reach, part] = grad_v[at:]
 
 
-def diagonal(blocks):
-    zero = jnp.zeros((HD, HD), BF16)
-    rows = [
-        jnp.concatenate([block.astype(BF16) if h == at else zero for h in range(len(blocks))], axis=1)
-        for at, block in enumerate(blocks)
-    ]
-    return jnp.concatenate(rows, axis=0)
-
-
 def split(blocks):
-    low = [block - block.astype(BF16).astype(F32) for block in blocks]
-    return diagonal(blocks), diagonal(low)
+    high = [block.astype(BF16) for block in blocks]
+    return [(top, (block - top.astype(F32)).astype(BF16)) for block, top in zip(blocks, high)]
 
 
 def split_dot(rows, state, contract):
-    return dot(rows, state[0], contract) + dot(rows, state[1], contract)
+    out = []
+    for h, parts in enumerate(state):
+        left = rows[:, h * HD : (h + 1) * HD]
+        out.append(dot(jnp.concatenate([left, left], axis=1), jnp.concatenate(parts, axis=contract[1][0]), contract))
+    return jnp.concatenate(out, axis=1)
 
 
 def outer_kernel(gates_ref, begin_ref, scaled_ref, k_ref, v_ref, g_ref, *refs):
@@ -244,10 +239,10 @@
         returning = [state + after * slot_ref[h] for h, state in enumerate(returning)]
     entering, returning = split(entering), split(returning)
     copies = [pltpu.make_async_copy(out_refs[at], out_hbms[at], sems.at[at]) for at in range(4)]
+    scales = jnp.concatenate([row_scales(begin_ref[...])] * heads, axis=1)
     attended = inner_refs[0][...] + split_dot(scaled_ref[...], entering, ((1,), (0,)))
     out_refs[0][...] = attended.astype(BF16)
     copies[0].start()
-    scales = jnp.concatenate([row_scales(begin_ref[...])] * heads, axis=1)
     grad_q = inner_refs[1][...] + split_dot(g_ref[...], entering, ((1,), (1,)))
     out_refs[1][...] = (scales * grad_q).astype(BF16)
     copies[1].start()
@@ -273,11 +268,16 @@
     state = jax.ShapeDtypeStruct((heads, HD, HD), F32)
     flat = jax.ShapeDtypeStruct((rows, width), BF16)
     partial = jax.ShapeDtypeStruct((rows, width), F32)
-    kinds = [(1, "odd"), (reach, "upper"), (reach, "lower")] + [(reach - 1, "relay")] + [(2, "ring")] + [(steps, "odd") for steps in range(4, reach - 1, 2)] + [(steps, "even") for steps in range(1, reach - 1, 2)]
-    rows_of = lambda n, kind: jax.ShapeDtypeStruct((n, HD), kind)
+    far_kinds = [(1, "odd"), (reach, "upper"), (reach, "lower")]
+    near_kinds = [(reach - 1, "relay"), (2, "ring")]
+    near_kinds += [(steps, "odd") for steps in range(4, reach - 1, 2)]
+    near_kinds += [(steps, "even") for steps in range(1, reach - 1, 2)]
+    kinds = tuple(far_kinds + near_kinds)
+    row_flags = [jax.ShapeDtypeStruct((n, HD), F32) for n in (3, 2 * len(kinds))]
+    row_values = [jax.ShapeDtypeStruct((rows, HD), kind) for kind in (F32, jnp.int32)]
     other, left, right, own_left, own_right, weight, begin, flags, gates = pl.pallas_call(
-        functools.partial(trade_kernel, tuple(kinds), reach),
-        out_shape=(state,) + (flat,) * 4 + (rows_of(rows, F32), rows_of(rows, jnp.int32), rows_of(3, F32), rows_of(2 * len(kinds), F32)),
+        functools.partial(trade_kernel, kinds, reach),
+        out_shape=(state, *(flat,) * 4, *row_values, *row_flags),
         in_specs=[HBM] * 5,
         out_specs=[VMEM] * 9,
         scratch_shapes=[pltpu.SMEM((docs,), jnp.int32), pltpu.SemaphoreType.DMA((5,))],
@@ -295,24 +295,20 @@
         cost_estimate=pl.CostEstimate(flops=2 * rows * width * width, bytes_accessed=2 * rows * width * 2, transcendentals=0),
         name="kept_state",
     )(own_left, own_right, weight, other)
-    far = [
-        (reach, "upper", send(even, group_pairs(count, reach, 0))),
-        (reach, "lower", send(odd, group_pairs(count, reach, 1))),
-    ]
-    joined = own + flags[0] * mate
-    joined = lax.optimization_barrier(joined)
-    ringed = jnp.where(flags[2] > 0.5, far[0][2], joined)
-    high_far, _ = lax.optimization_barrier((far[1][2], ringed))
-    relayed = jnp.where(flags[1] > 0.5, far[0][2], high_far)
-    near = [
-        (reach - 1, "relay", send(relayed, mate_pairs(count)[2:-2])),
-        (2, "ring", send(ringed, ring_pairs(count, 2, True))),
-        *[(steps, "odd", send(joined, ring_pairs(count, steps, True))) for steps in range(4, reach - 1, 2)],
-        *[(steps, "even", send(joined, swap_pairs(count, steps))) for steps in range(1, reach - 1, 2)],
-    ]
-    slots = [(1, "odd", mate)] + far + near
-    received = [value for _, _, value in slots]
-    assert kinds == [(steps, kind) for steps, kind, _ in slots]
+    upward = send(even, group_pairs(count, reach, 0))
+    downward = send(odd, group_pairs(count, reach, 1))
+    joined = lax.optimization_barrier(own + flags[0] * mate)
+    ringed = jnp.where(flags[2] > 0.5, upward, joined)
+    late, _ = lax.optimization_barrier((downward, ringed))
+    relayed = jnp.where(flags[1] > 0.5, upward, late)
+    received = [mate, upward, downward]
+    for steps, kind in near_kinds:
+        if kind == "relay":
+            received.append(send(relayed, mate_pairs(count)[2:-2]))
+        elif kind == "even":
+            received.append(send(joined, swap_pairs(count, steps)))
+        else:
+            received.append(send(ringed if kind == "ring" else joined, ring_pairs(count, steps)))
     tensors = pl.pallas_call(
         inner_kernel,
         out_shape=(flat,) * 4 + (partial,) * 4,
@@ -325,7 +321,7 @@
     return pl.pallas_call(
         outer_kernel,
         out_shape=(flat,) * 4,
-        in_specs=[VMEM] * (10 + len(slots)),
+        in_specs=[VMEM] * (10 + len(received)),
         out_specs=[HBM] * 4,
         scratch_shapes=[pltpu.VMEM((rows, width), BF16)] * 4 + [pltpu.SemaphoreType.DMA((4,))],
         compiler_params=params,

time: 18.3 us -> 18.2 us (level)
  no operation moved by 1% of the time
where the time goes in v7:
time: 18.2 us; the launch traced here: 17.8 us
  starting transfers between devices  6.33 us (35%)
  waiting for transfers between devices  5.72 us (31%)
  Pallas kernels  5 us (27%)
  between operations  0.71 us (4%)
    ppermute x6, starting transfers between devices, send(): return lax.ppermute(value, ('ctx', 'head'), wide)  6.33 us
    ppermute x6, waiting for transfers between devices, send(): return lax.ppermute(value, ('ctx', 'head'), wide)  5.72 us
    pallas_call x1, Pallas kernels, body(): pl.pallas_call(inner_kernel, out_shape=(flat,) * 4 + (partial,) * 4, in_s...  1.85 us
    pallas_call x1, Pallas kernels, body(): pl.pallas_call(outer_kernel, out_shape=(flat,) * 4, in_specs=[VMEM] * (10...  1.5 us
    pallas_call x1, Pallas kernels, body(): pl.pallas_call(functools.partial(trade_kernel, kinds, reach), out_shape=(...  1.37 us
  transfers between devices with their start and end apart: 6, of which 3 were waited for; matrix products, arithmetic and copies ran while one was open for 0% of the time, Pallas kernels for 12%

profile of v7, /device:TPU:0, one launch (start us, length us, event | category | flops | bytes accessed | tf_op | source)
XLA Modules:
  0.0 17.8 jit_solution(2893457659149110384)
XLA Ops:
  0.6 1.4 %traded_state.1 = (f32[2,128,128]{2,1,0:T(8,128)S(1)}, bf16[512,256]{1,0:T(8,128)(2,1)S(1)}, bf16[512,256]{1,0:T(8,128)(2,1)S(1)}, bf16[512,256]{1,0:T(8,128)(2,...) custom-call(s32[8]{0:T(128)} %lengths_hbm.1, ...), custom_call_target="tpu_custom_call" | custom-call | flops 67108864 | bytes 1048576 | tf_op jit(solution)/shard_map/traded_state/pallas_call | solution.py:278
  2.0 3.0 %collective-permute-start = (f32[2,128,128]{2,1,0:T(8,128)S(1)}, f32[2,128,128]{2,1,0:T(8,128)S(1)}, u32[]{:S(2)}, u32[]{:S(2)}) collective-permute-start(f32[2,128,128]{2,1,0:T(8,128)S(1)} %get-tuple-element.39.other_ref), channel_id=1, source_target_pairs={{0,2},{1,3},{2,0},{3,1},{4,6},{5,7},{6,4},{7,5},{8,10},{9,11},{10,... | collective-permute-start | bytes 393224 | tf_op jit(solution)/shard_map/ppermute | solution.py:47
  5.0 0.3 %kept_state.1 = (f32[2,128,128]{2,1,0:T(8,128)S(1)}, f32[2,128,128]{2,1,0:T(8,128)S(1)}, f32[2,128,128]{2,1,0:T(8,128)S(1)}) custom-call(bf16[512,256]{1,0:T(8,128)(2,1)S(1)} %get-tuple-element.29.own_left_ref.left_ref, bf16[512,256]{1,0:T(8,128)(2,1)S(1)} %get-tuple-element.30.own_right_ref.right_ref, f32[512,128]{1,0:T(8,128)S(1)} %get-tuple-element.40.weight_ref, ...), custom_call_target="tpu_custom_call" | custom-call | flops 67108864 | bytes 524288 | tf_op jit(solution)/shard_map/kept_state/pallas_call | solution.py:289
  5.3 1.6 %collective-permute-start.1 = (f32[2,128,128]{2,1,0:T(8,128)S(1)}, f32[2,128,128]{2,1,0:T(8,128)S(1)}, u32[]{:S(2)}, u32[]{:S(2)}) collective-permute-start(f32[2,128,128]{2,1,0:T(8,128)S(1)} %get-tuple-element.41), channel_id=1, source_target_pairs={{0,8},{1,9},{2,10},{3,11},{4,12},{5,13},{6,14},{7,15},{16,24},{17,... | collective-permute-start | bytes 393224 | tf_op jit(solution)/shard_map/ppermute | solution.py:47
  6.9 0.0 collective-permute-start.2
  7.0 1.5 %collective-permute-done.refs_4_ = f32[2,128,128]{2,1,0:T(8,128)S(1)} collective-permute-done((f32[2,128,128]{2,1,0:T(8,128)S(1)}, f32[2,128,128]{2,1,0:T(8,128)S(1)}, u32[]{:S(2)}, u32[]{:S(2)}) %collective-permute-start) | collective-permute-done | bytes 131104 | tf_op jit(solution)/shard_map/ppermute | solution.py:47
  8.5 0.1 collective-permute-start.5
  8.6 1.7 %collective-permute-done.1.refs_5_ = f32[2,128,128]{2,1,0:T(8,128)S(1)} collective-permute-done((f32[2,128,128]{2,1,0:T(8,128)S(1)}, f32[2,128,128]{2,1,0:T(8,128)S(1)}, u32[]{:S(2)}, u32[]{:S(2)}) %collective-permute-start.1) | collective-permute-done | bytes 131104 | tf_op jit(solution)/shard_map/ppermute | solution.py:47
  10.4 1.5 %collective-permute-start.4 = (f32[2,128,128]{2,1,0:T(8,128)S(1)}, f32[2,128,128]{2,1,0:T(8,128)S(1)}, u32[]{:S(2)}, u32[]{:S(2)}) collective-permute-start(f32[2,128,128]{2,1,0:T(8,128)S(1)} %broadcast_select_fusion), channel_id=1, source_target_pairs={{0,2},{1,3},{2,6},{3,7},{4,0},{5,1},{6,10},{7,11},{8,4},{9,5},{10,... | collective-permute-start | bytes 393224 | tf_op jit(solution)/shard_map/ppermute | solution.py:47
  11.9 0.0 collective-permute-done.2.refs_6_
  11.9 0.1 collective-permute-start.3
  12.0 1.8 %within_block.1 = (bf16[512,256]{1,0:T(8,128)(2,1)S(1)}, bf16[512,256]{1,0:T(8,128)(2,1)S(1)}, bf16[512,256]{1,0:T(8,128)(2,1)S(1)}, bf16[512,256]{1,0:T(8,128)(...) custom-call(bf16[512,256]{1,0:T(8,128)(2,1)S(1)} %get-tuple-element., ...), custom_call_target="tpu_custom_call" | custom-call | flops 805306368 | bytes 3145728 | tf_op jit(solution)/shard_map/within_block/pallas_call | solution.py:312
  13.9 0.0 collective-permute-done.5.refs_9_
  13.9 2.4 %collective-permute-done.4.refs_8_ = f32[2,128,128]{2,1,0:T(8,128)S(1)} collective-permute-done((f32[2,128,128]{2,1,0:T(8,128)S(1)}, f32[2,128,128]{2,1,0:T(8,128)S(1)}, u32[]{:S(2)}, u32[]{:S(2)}) %collective-permute-start.4) | collective-permute-done | bytes 131104 | tf_op jit(solution)/shard_map/ppermute | solution.py:47
  16.3 0.0 collective-permute-done.3.refs_7_
  16.3 1.5 %across_blocks.1 = (bf16[512,256]{1,0:T(8,128)(2,1)}, bf16[512,256]{1,0:T(8,128)(2,1)}, bf16[512,256]{1,0:T(8,128)(2,1)}, bf16[512,256]{1,0:T(8,128)(2,1)}) custom-call(f32[12,128]{1,0:T(8,128)S(1)} %get-tuple-element.25.gates_ref, s32[512,128]{1,0:T(8,128)S(1)} %get-tuple-element.26.begin_ref, bf16[512,256]{1,0:T(8,128)(2,1)S(1)} %get-tuple-element.31.scaled_ref, ...), custom_call_target="tpu_custom_call" | custom-call | flops 134217728 | bytes 4194304 | tf_op jit(solution)/shard_map/across_blocks/pallas_call | solution.py:321
  (5 shorter events, 0.1 us)
Async XLA Ops:
  2.0 6.5 %collective-permute-start = (f32[2,128,128]{2,1,0:T(8,128)S(1)}, f32[2,128,128]{2,1,0:T(8,128)S(1)}, u32[]{:S(2)}, u32[]{:S(2)}) collective-permute-start(f32[2,128,128]{2,1,0:T(8,128)S(1)} %get-tuple-element.39.other_ref), channel_id=1, source_target_pairs={{0,2},{1,3},{2,0},{3,1},{4,6},{5,7},{6,4},{7,5},{8,10},{9,11},{10,... | collective-permute-start | bytes 393224 | tf_op jit(solution)/shard_map/ppermute | solution.py:47
  5.3 5.0 %collective-permute-start.1 = (f32[2,128,128]{2,1,0:T(8,128)S(1)}, f32[2,128,128]{2,1,0:T(8,128)S(1)}, u32[]{:S(2)}, u32[]{:S(2)}) collective-permute-start(f32[2,128,128]{2,1,0:T(8,128)S(1)} %get-tuple-element.41), channel_id=1, source_target_pairs={{0,8},{1,9},{2,10},{3,11},{4,12},{5,13},{6,14},{7,15},{16,24},{17,... | collective-permute-start | bytes 393224 | tf_op jit(solution)/shard_map/ppermute | solution.py:47
  6.9 5.0 %collective-permute-start.2 = (f32[2,128,128]{2,1,0:T(8,128)S(1)}, f32[2,128,128]{2,1,0:T(8,128)S(1)}, u32[]{:S(2)}, u32[]{:S(2)}) collective-permute-start(f32[2,128,128]{2,1,0:T(8,128)S(1)} %get-tuple-element.42), channel_id=1, source_target_pairs={{8,16},{9,17},{10,18},{11,19},{12,20},{13,21},{14,22},{15,23},{16,... | collective-permute-start | bytes 393224 | tf_op jit(solution)/shard_map/ppermute | solution.py:47
  8.5 5.3 %collective-permute-start.5 = (f32[2,128,128]{2,1,0:T(8,128)S(1)}, f32[2,128,128]{2,1,0:T(8,128)S(1)}, u32[]{:S(2)}, u32[]{:S(2)}) collective-permute-start(f32[2,128,128]{2,1,0:T(8,128)S(1)} %multiply_add_fusion), channel_id=1, source_target_pairs={{2,4},{3,5},{6,8},{7,9},{10,12},{11,13},{14,16},{15,17},{18,20},{1... | collective-permute-start | bytes 393224 | tf_op jit(solution)/shard_map/ppermute | solution.py:47
  10.4 6.0 %collective-permute-start.4 = (f32[2,128,128]{2,1,0:T(8,128)S(1)}, f32[2,128,128]{2,1,0:T(8,128)S(1)}, u32[]{:S(2)}, u32[]{:S(2)}) collective-permute-start(f32[2,128,128]{2,1,0:T(8,128)S(1)} %broadcast_select_fusion), channel_id=1, source_target_pairs={{0,2},{1,3},{2,6},{3,7},{4,0},{5,1},{6,10},{7,11},{8,4},{9,5},{10,... | collective-permute-start | bytes 393224 | tf_op jit(solution)/shard_map/ppermute | solution.py:47
  11.9 4.4 %collective-permute-start.3 = (f32[2,128,128]{2,1,0:T(8,128)S(1)}, f32[2,128,128]{2,1,0:T(8,128)S(1)}, u32[]{:S(2)}, u32[]{:S(2)}) collective-permute-start(f32[2,128,128]{2,1,0:T(8,128)S(1)} %broadcast_select_fusion.1), channel_id=1, source_target_pairs={{4,6},{5,7},{6,4},{7,5},{8,10},{9,11},{10,8},{11,9},{12,14},{13,15... | collective-permute-start | bytes 393224 | tf_op jit(solution)/shard_map/ppermute | solution.py:47
